TPU v7x, 32 devices: a whole 2x2x4 slice. The times are simulated.
32 devices in a mesh: row: 4 (over y, x), col: 8 (over z, core).
Axes of the slice: x: 2, y: 2, z: 4, core: 2. Of those that a mesh axis runs over, the one named last changes fastest.
Arguments:
- covariates: bfloat16 [32768, 4096], P('row', 'col'), may hold values from -64 to 64
- labels: int32 [32768], P('row'), may hold values from 0 to 15
- weights: float32 [16, 4096], P(None, 'col'), may hold values from -0.0234375 to 0.0234375
- sample_index: int32 [16384], P('row'), may hold values from 0 to 32767, as said below
Outputs:
- gradient: float32 [16, 4096], P(None, 'col')
- newton_step: float32 [16, 4096], P(None, 'col')
Inputs may be any that keep to these rules, and one draw needn't show every extreme that they name: The 4096 entries sample_index[b * 4096] to sample_index[(b + 1) * 4096 - 1] name users b * 8192 to (b + 1) * 8192 - 1; repeats may occur.
All inputs are finite; a program needn't handle non-finite values.
Results may differ from a plain program's by a relative error of at most 0.0039.
Values may be sent and summed in bfloat16 or wider, within the bound.
A program may use at most 64 MiB of HBM per device.

v0:
```python
import jax
import jax.numpy as jnp
from jax import lax
from jax.sharding import PartitionSpec as P

ITERS = 2


RIDGE_WEIGHT = 0.004


def class_shares(logits):
    exponent = jnp.exp(logits)
    return exponent / jnp.sum(exponent, axis=0, keepdims=True)


def body(covariates, labels, weights, sample_index):
    user_rows = covariates.shape[0]
    col_width = covariates.shape[1]
    row_count = lax.axis_size("row")
    sub_rows_dev = sample_index.shape[0]
    first_user = lax.axis_index("row") * user_rows
    own_width = col_width // row_count
    own_start = lax.axis_index("row") * own_width
    rounded_weights = weights.astype(jnp.bfloat16)
    within = sample_index - first_user
    sub_rows = jnp.take(covariates, within, axis=0)
    partial_value = lax.dot_general(
        rounded_weights, covariates, (((1,), (1,)), ((), ())), preferred_element_type=jnp.float32
    )
    logits = lax.psum(partial_value, "col")
    shares = class_shares(logits)
    classes = lax.broadcasted_iota(jnp.int32, shares.shape, 0)
    indicator = (labels[None, :] == classes).astype(jnp.float32)
    misfit = (shares - indicator).astype(jnp.bfloat16)
    sub_shares = jnp.take(shares, within, axis=1)
    grad_term = jnp.dot(misfit, covariates, preferred_element_type=jnp.float32)
    gradient = lax.psum(grad_term, "row") / (user_rows * row_count) + RIDGE_WEIGHT * weights
    sub_total = sub_rows_dev * row_count

    def own_columns(vector):
        return lax.dynamic_slice_in_dim(vector, own_start, own_width, 1)

    def local_inner(first_vec, second_vec):
        return jnp.sum(own_columns(first_vec) * own_columns(second_vec))

    residual = -gradient
    direction = residual
    newton_step = jnp.zeros_like(residual)
    norm_now = lax.psum(local_inner(residual, residual), ("row", "col"))
    for iteration in range(ITERS):
        rounded = direction.astype(jnp.bfloat16)
        partial_response = lax.dot_general(
            rounded, sub_rows, (((1,), (1,)), ((), ())), preferred_element_type=jnp.float32
        )
        response = lax.psum(partial_response, "col")
        centred = response - jnp.sum(sub_shares * response, axis=0, keepdims=True)
        weighted = (sub_shares * centred).astype(jnp.bfloat16)
        summed = lax.psum(jnp.dot(weighted, sub_rows, preferred_element_type=jnp.float32), "row")
        image = summed / sub_total + RIDGE_WEIGHT * direction
        curve = lax.psum(local_inner(direction, image), ("row", "col"))
        step_size = norm_now / curve
        newton_step = newton_step + step_size * direction
        residual = residual - step_size * image
        if iteration + 1 < ITERS:
            norm_new = lax.psum(local_inner(residual, residual), ("row", "col"))
            direction = residual + norm_new / norm_now * direction
            norm_now = norm_new
    return (gradient, newton_step)


def solution(mesh):
    in_specs = (P("row", "col"), P("row"), P(None, "col"), P("row"))
    out_specs = (P(None, "col"), P(None, "col"))
    return jax.shard_map(body, mesh=mesh, in_specs=in_specs, out_specs=out_specs, check_vma=False)
```

profile of v0, /device:TPU:0, one launch (start us, length us, event | category | flops | bytes accessed | tf_op | source)
XLA Modules:
  0.0 381.7 jit_solution(12853045014525428970)
XLA Ops:
  7.2 0.0 all-reduce.5.cloned.1.call-start
  7.2 6.5 %fusion.20 = f32[16,8192]{1,0:T(8,128)} fusion(bf16[8192,512]{1,0:T(8,128)(2,1)} %param.4, f32[16,512]{1,0:T(8,128)} %param.6), kind=kOutput, calls=%fused_computation.35 | convolution fusion | flops 134225920 | bytes 8945664 | tf_op jit(solution)/shard_map/dot_general | solution.py:28
  13.7 0.0 all-reduce.5.cloned.1.call-update
  13.8 0.0 all-reduce.7.cloned.1.call-start
  13.9 21.8 %gather_fusion.1 = bf16[4096,512]{1,0:T(8,128)(2,1)} fusion(bf16[8192,512]{1,0:T(8,128)(2,1)} %param.4, s32[4096]{0:T(1024)S(1)} %fusion.22), kind=kCustom, calls=%fused_computation.1 | custom fusion | bytes 8404992 | tf_op jit(solution)/shard_map/jit(_take)/gather | solution.py:27
  35.7 37.0 %all-reduce.5.cloned.1.call-done = f32[16,8192]{1,0:T(8,128)} async-done(((f32[16,8192]{1,0:T(8,128)}), f32[16,8192]{1,0:T(8,128)}) %all-reduce.5.cloned.1.call-update) | async-done | bytes 524304 | tf_op jit(solution)/shard_map/psum | solution.py:31
  72.8 1.2 exponential_reduce_fusion
  73.9 1.2 exponential_divide_fusion
  75.1 4.6 %fusion = f32[16,512]{1,0:T(8,128)S(1)} fusion(bf16[8192,512]{1,0:T(8,128)(2,1)} %param.4, f32[16,8192]{1,0:T(8,128)S(1)} %exponential_divide_fusion, s32[8192]{0:T(1024)S(1)} %copy-done.3), kind=kOutput, calls=%fused_computation.7 | convolution fusion | flops 134742016 | bytes 8978432 | tf_op jit(solution)/shard_map/dot_general | solution.py:37
  79.7 16.2 %psum.71 = f32[16,512]{1,0:T(8,128)S(1)} all-reduce(f32[16,512]{1,0:T(8,128)S(1)} %fusion), channel_id=1, replica_groups=mesh['row'=4,'col'=8] {'row'}, use_global_device_ids=true, to_apply=%region_2.3 | all-reduce | flops 8192 | bytes 65536 | tf_op jit(solution)/shard_map/psum | solution.py:38
  95.9 3.7 fusion.18
  99.7 0.0 all-reduce.7.cloned.1.call-update
  99.7 0.0 all-reduce.9.cloned.1.call-start
  99.8 2.7 copy.6
  102.4 13.0 %gather_fusion = f32[4096,16]{1,0:T(8,128)S(1)} fusion(f32[16,8192]{0,1:T(8,128)} %copy.6, s32[4096]{0:T(1024)S(1)} %fusion.22), kind=kCustom, calls=%fused_computation | custom fusion | bytes 540672 | tf_op jit(solution)/shard_map/jit(_take)/gather | solution.py:36
  115.4 0.6 copy.7
  115.9 36.1 %all-reduce.7.cloned.1.call-done = f32[16,4096]{1,0:T(8,128)} async-done(((f32[16,4096]{1,0:T(8,128)}), f32[16,4096]{1,0:T(8,128)}) %all-reduce.7.cloned.1.call-update) | async-done | bytes 262160 | tf_op jit(solution)/shard_map/psum | solution.py:56
  152.0 1.0 fusion.1
  153.0 2.8 fusion.8
  155.9 16.2 %psum.74 = f32[16,512]{1,0:T(8,128)S(1)} all-reduce(f32[16,512]{1,0:T(8,128)S(1)} %fusion.8), channel_id=1, replica_groups=mesh['row'=4,'col'=8] {'row'}, use_global_device_ids=true, to_apply=%region_7.8 | all-reduce | flops 8192 | bytes 65536 | tf_op jit(solution)/shard_map/psum | solution.py:59
  172.1 0.6 multiply_reduce_fusion.1
  172.7 38.5 %all-reduce = (f32[]{:T(128)}, f32[]{:T(128)}) all-reduce(f32[]{:T(128)} %get-tuple-element.3, f32[]{:T(128)} %get-tuple-element.2), channel_id=1, replica_groups=mesh['row'=4,'col'=8] {'row','col'}, use_global_device_ids=true, to_apply=%region_4.5 | all-reduce | flops 2 | bytes 16 | tf_op jit(solution)/shard_map/psum | solution.py:50
  212.6 0.6 multiply_reduce_fusion
  213.2 40.4 %psum.76 = f32[]{:T(128)} all-reduce(f32[]{:T(128)} %multiply_reduce_fusion), channel_id=1, replica_groups=mesh['row'=4,'col'=8] {'row','col'}, use_global_device_ids=true, to_apply=%region_11.12 | all-reduce | flops 1 | bytes 8 | tf_op jit(solution)/shard_map/psum | solution.py:66
  254.9 3.7 fusion.16
  258.7 55.2 %all-reduce.9.cloned.1.call-done = f32[16,4096]{1,0:T(8,128)} async-done(((f32[16,4096]{1,0:T(8,128)}), f32[16,4096]{1,0:T(8,128)}) %all-reduce.9.cloned.1.call-update) | async-done | bytes 262160 | tf_op jit(solution)/shard_map/psum | solution.py:56
  313.9 1.0 fusion.3
  314.9 2.8 fusion.6
  317.7 16.2 %psum.78 = f32[16,512]{1,0:T(8,128)S(1)} all-reduce(f32[16,512]{1,0:T(8,128)S(1)} %fusion.6), channel_id=1, replica_groups=mesh['row'=4,'col'=8] {'row'}, use_global_device_ids=true, to_apply=%region_14.15 | all-reduce | flops 8192 | bytes 65536 | tf_op jit(solution)/shard_map/psum | solution.py:59
  334.0 0.7 fusion.25
  334.6 38.5 %psum.79 = f32[]{:T(128)} all-reduce(f32[]{:T(128)} %fusion.25), channel_id=1, replica_groups=mesh['row'=4,'col'=8] {'row','col'}, use_global_device_ids=true, to_apply=%region_16.17 | all-reduce | flops 1 | bytes 8 | tf_op jit(solution)/shard_map/psum | solution.py:61
  374.5 0.6 multiply_add_fusion
  (15 shorter events, 0.1 us)
Async XLA Ops:
  7.2 6.7 %copy-start.2 = (s32[4096]{0:T(1024)S(1)}, s32[4096]{0:T(1024)}, u32[]{:S(2)}) copy-start(s32[4096]{0:T(1024)} %param.7) | copy-start | bytes 49156
  7.2 65.6 %all-reduce.5.cloned.1.call-start = ((), (), s32[]{:S(2)}) async-start(), calls=%async_computation | async-start | bytes 1048576 | tf_op jit(solution)/shard_map/psum | solution.py:31
  13.8 138.3 %all-reduce.7.cloned.1.call-start = ((), (), s32[]{:S(2)}) async-start(), calls=%async_computation.1 | async-start | bytes 524288 | tf_op jit(solution)/shard_map/psum | solution.py:56
  13.8 61.2 %copy-start.3 = (s32[8192]{0:T(1024)S(1)}, s32[8192]{0:T(1024)}, u32[]{:S(2)}) copy-start(s32[8192]{0:T(1024)} %param.5) | copy-start | bytes 98308
  75.1 20.8 %copy-start.1 = (f32[16,512]{1,0:T(8,128)S(1)}, f32[16,512]{1,0:T(8,128)}, u32[]{:S(2)}) copy-start(f32[16,512]{1,0:T(8,128)} %param.6) | copy-start | bytes 98308
  95.9 278.6 %copy-start = (f32[16,512]{1,0:T(8,128)}, f32[16,512]{1,0:T(8,128)S(1)}, u32[]{:S(2)}) copy-start(f32[16,512]{1,0:T(8,128)S(1)} %get-tuple-element.7) | copy-start | bytes 98308
  99.7 214.2 %all-reduce.9.cloned.1.call-start = ((), (), s32[]{:S(2)}) async-start(), calls=%async_computation.2 | async-start | bytes 524288 | tf_op jit(solution)/shard_map/psum | solution.py:56
Sparse Core Ops, SparseCore 0:
  13.9 58.8 all-reduce.4
  99.8 52.1 all-reduce.6
  258.8 55.0 all-reduce.8
where the time goes:
time: 382 us
  blocking collectives  166 us (43%)
  waiting for transfers between devices  128 us (34%)
  local copies, waits for them, and re-layouts  38.1 us (10%)
  matrix products  24.2 us (6%)
  between operations  17.9 us (5%)
  other arithmetic  6.95 us (2%)
    psum x2, waiting for transfers between devices, body(): response = lax.psum(partial_response, 'col')  91.3 us
    psum x1, blocking collectives, body(): norm_new = lax.psum(local_inner(residual, residual), ('row', 'col'))  40.4 us
    psum x1, blocking collectives, body(): norm_now = lax.psum(local_inner(residual, residual), ('row', 'col'))  38.5 us
    psum x1, blocking collectives, body(): curve = lax.psum(local_inner(direction, image), ('row', 'col'))  38.5 us
    psum x1, waiting for transfers between devices, body(): logits = lax.psum(partial_value, 'col')  37 us
    psum x2, blocking collectives, body(): lax.psum(jnp.dot(weighted, sub_rows, preferred_element_type=jnp.float32),...  32.5 us
    gather x1, local copies, waits for them, and re-layouts, body(): sub_rows = jnp.take(covariates, within, axis=0)  21.8 us
    psum x1, blocking collectives, body(): lax.psum(grad_term, 'row') / (user_rows * row_count)  16.2 us
  transfers between devices with their start and end apart: 3, of which 3 were waited for; matrix products, arithmetic and copies ran while one was open for 10% of the time, Pallas kernels for 0%

commit v1 on v0

v1 whole, which is shorter than its diff:
```python
import functools

import jax
import jax.numpy as jnp
from jax import lax
from jax.experimental import pallas as pl
from jax.experimental.pallas import tpu as pltpu
from jax.sharding import PartitionSpec as P

ITERS = 2
RIDGE_WEIGHT = 0.004
LANES = 128
MESH = pl.DeviceIdType.MESH


def fold(value):
    value = value[:8] + value[8:]
    total = value[:, :LANES]
    for start in range(LANES, value.shape[1], LANES):
        total = total + value[:, start:start + LANES]
    return total


def kernel(
    n, rows, user_total, sub_total,
    cov_hbm, labels_ref, weights_ref, index_ref, gradient_ref, step_ref,
    cov, logit_send, logit_recv, resp_send, resp_recv, share_send, share_recv, row_buf, dot_send, dot_recv,
    cov_sem, rs_ssem, rs_rsem, ag_ssem, ag_rsem, row_ssem, row_rsem, dot_ssem, dot_rsem,
):
    me = lax.axis_index("col")
    my_row = lax.axis_index("row")
    chips = n // 2
    own = cov.shape[1]
    classes = weights_ref.shape[0]

    def target(j):
        return lax.rem(me // 2 + j // 2, chips) * 2 + lax.rem(lax.rem(me, 2) + lax.rem(j, 2), 2)

    def source(j):
        return lax.rem(me // 2 + chips - j // 2, chips) * 2 + lax.rem(lax.rem(me, 2) + 2 - lax.rem(j, 2), 2)

    def cov_copy(j):
        block = target(j)
        return pltpu.make_async_copy(cov_hbm.at[block], cov.at[block], cov_sem.at[j])

    def start_cov(i, carry):
        cov_copy(n - 1 - i).start()
        return carry

    lax.fori_loop(0, n, start_cov, 0)

    barrier = pltpu.get_barrier_semaphore()

    def greet_col(j, carry):
        pl.semaphore_signal(barrier, inc=1, device_id={"col": target(j)}, device_id_type=MESH)
        return carry

    def greet_row(t, carry):
        pl.semaphore_signal(
            barrier, inc=1, device_id={"row": lax.rem(my_row + t, rows)}, device_id_type=MESH
        )
        return carry

    lax.fori_loop(1, n, greet_col, 0)
    lax.fori_loop(1, rows, greet_row, 0)

    groups = own // LANES
    padded = max(16, groups)
    within = index_ref[...] - my_row * (n * own) - me * own
    lane = jnp.bitwise_and(within, LANES - 1)
    group = jnp.right_shift(within - lane, 7)
    group_hot = (lax.broadcasted_iota(jnp.int32, (padded, within.shape[1]), 0) == group)
    lane_hot = (lax.broadcasted_iota(jnp.int32, (LANES, within.shape[1]), 0) == lane)
    counts = lax.dot_general(
        group_hot.astype(jnp.float32).astype(jnp.bfloat16), lane_hot.astype(jnp.float32).astype(jnp.bfloat16),
        (((1,), (1,)), ((), ())), preferred_element_type=jnp.float32,
    )
    count = jnp.concatenate([counts[g:g + 1] for g in range(groups)], axis=1)

    pl.semaphore_wait(barrier, n - 1 + rows - 1)

    def rs_copy(phase, send, recv, j):
        return pltpu.make_async_remote_copy(
            src_ref=send.at[j], dst_ref=recv.at[j],
            send_sem=rs_ssem.at[phase, j], recv_sem=rs_rsem.at[phase, j],
            device_id={"col": target(j)}, device_id_type=MESH,
        )

    def project(vector, block):
        return lax.dot_general(
            vector, cov[block], (((1,), (1,)), ((), ())), preferred_element_type=jnp.float32
        )

    def reduce_users(phase, vector, send, recv):
        def one(i, carry):
            j = n - 1 - i
            if phase == 0:
                cov_copy(j).wait()
            send[j] = project(vector, target(j)).astype(send.dtype)
            rs_copy(phase, send, recv, j).start()
            return carry

        lax.fori_loop(0, n - 1, one, 0)
        if phase == 0:
            cov_copy(0).wait()

        def add(j, total):
            rs_copy(phase, send, recv, j).wait_recv()
            return total + recv[j].astype(jnp.float32)

        return lax.fori_loop(1, n, add, project(vector, me))

    def ag_copy(phase, j):
        return pltpu.make_async_remote_copy(
            src_ref=share_send.at[phase], dst_ref=share_recv.at[phase, j],
            send_sem=ag_ssem.at[phase, j], recv_sem=ag_rsem.at[phase, j],
            device_id={"col": target(j)}, device_id_type=MESH,
        )

    def row_copy(phase, t, slot):
        return pltpu.make_async_remote_copy(
            src_ref=row_buf.at[phase, my_row], dst_ref=row_buf.at[phase, slot],
            send_sem=row_ssem.at[phase, t], recv_sem=row_rsem.at[phase, t],
            device_id={"row": lax.rem(my_row + t, rows)}, device_id_type=MESH,
        )

    def back_project(phase, values):
        share_send[phase] = values

        def send(j, carry):
            ag_copy(phase, j).start()
            return carry

        lax.fori_loop(1, n, send, 0)

        def add(j, total):
            ag_copy(phase, j).wait_recv()
            return total + jnp.dot(
                share_recv[phase, j], cov[source(j)], preferred_element_type=jnp.float32
            )

        row_buf[phase, my_row] = lax.fori_loop(
            1, n, add, jnp.dot(values, cov[me], preferred_element_type=jnp.float32)
        )

        def send_row(t, carry):
            row_copy(phase, t, my_row).start()
            return carry

        def wait_row(t, carry):
            row_copy(phase, t, lax.rem(my_row + rows - t, rows)).wait_recv()
            return carry

        lax.fori_loop(1, rows, send_row, 0)
        lax.fori_loop(1, rows, wait_row, 0)
        total = row_buf[phase, 0]
        for r in range(1, rows):
            total = total + row_buf[phase, r]
        return total

    def dot_copy(phase, j):
        return pltpu.make_async_remote_copy(
            src_ref=dot_send.at[phase], dst_ref=dot_recv.at[phase, j],
            send_sem=dot_ssem.at[phase, j], recv_sem=dot_rsem.at[phase, j],
            device_id={"col": target(j)}, device_id_type=MESH,
        )

    def inner(phase, *pairs):
        for k, (first, second) in enumerate(pairs):
            dot_send[phase, k] = fold(first * second)

        def send(j, carry):
            dot_copy(phase, j).start()
            return carry

        def add(j, totals):
            dot_copy(phase, j).wait_recv()
            return tuple(total + dot_recv[phase, j, k] for k, total in enumerate(totals))

        lax.fori_loop(1, n, send, 0)
        totals = lax.fori_loop(1, n, add, tuple(dot_send[phase, k] for k in range(len(pairs))))
        return [jnp.sum(total, keepdims=True) for total in totals]

    weights = weights_ref[...]
    logits = reduce_users(0, weights.astype(jnp.bfloat16), logit_send, logit_recv)
    exponent = jnp.exp(logits)
    shares = exponent / jnp.sum(exponent, axis=0, keepdims=True)
    label = labels_ref[me]
    indicator = (label == lax.broadcasted_iota(jnp.int32, (classes, own), 0)).astype(jnp.float32)
    misfit = (shares - indicator).astype(jnp.bfloat16)
    gradient = back_project(0, misfit) / user_total + RIDGE_WEIGHT * weights
    gradient_ref[...] = gradient
    counted = count * shares

    residual = -gradient
    direction = residual
    newton_step = jnp.zeros_like(residual)
    norm_now = None
    for iteration in range(ITERS):
        response = reduce_users(
            iteration + 1, direction.astype(jnp.bfloat16), resp_send.at[iteration], resp_recv.at[iteration]
        )
        centred = response - jnp.sum(shares * response, axis=0, keepdims=True)
        weighted = (counted * centred).astype(jnp.bfloat16)
        image = back_project(iteration + 1, weighted) / sub_total + RIDGE_WEIGHT * direction
        if norm_now is None:
            curve, norm_now = inner(2 * iteration, (direction, image), (residual, residual))
        else:
            (curve,) = inner(2 * iteration, (direction, image))
        step_size = norm_now / curve
        newton_step = newton_step + step_size * direction
        residual = residual - step_size * image
        if iteration + 1 < ITERS:
            (norm_new,) = inner(2 * iteration + 1, (residual, residual))
            direction = residual + (norm_new / norm_now) * direction
            norm_now = norm_new
    step_ref[...] = newton_step

    def drain_col(j, carry):
        rs_copy(0, logit_send, logit_recv, j).wait_send()
        for phase in range(ITERS):
            rs_copy(phase + 1, resp_send.at[phase], resp_recv.at[phase], j).wait_send()
        for phase in range(ITERS + 1):
            ag_copy(phase, j).wait_send()
        for phase in range(2 * ITERS - 1):
            dot_copy(phase, j).wait_send()
        return carry

    def drain_row(t, carry):
        for phase in range(ITERS + 1):
            row_copy(phase, t, my_row).wait_send()
        return carry

    lax.fori_loop(1, n, drain_col, 0)
    lax.fori_loop(1, rows, drain_row, 0)


def body(covariates, labels, weights, sample_index):
    users, width = covariates.shape
    n, rows = lax.axis_size("col"), lax.axis_size("row")
    own = users // n
    classes = weights.shape[0]
    sub = sample_index.shape[0]
    dots = 2 * ITERS - 1
    dma = pltpu.SemaphoreType.DMA
    vmem = pl.BlockSpec(memory_space=pltpu.VMEM)
    return pl.pallas_call(
        functools.partial(kernel, n, rows, users * rows, sub * rows),
        out_shape=[jax.ShapeDtypeStruct((classes, width), jnp.float32)] * 2,
        in_specs=[pl.BlockSpec(memory_space=pl.ANY), vmem, vmem, vmem],
        out_specs=[vmem, vmem],
        scratch_shapes=[
            pltpu.VMEM((n, own, width), jnp.bfloat16),
            pltpu.VMEM((n, classes, own), jnp.float32),
            pltpu.VMEM((n, classes, own), jnp.float32),
            pltpu.VMEM((ITERS, n, classes, own), jnp.bfloat16),
            pltpu.VMEM((ITERS, n, classes, own), jnp.bfloat16),
            pltpu.VMEM((ITERS + 1, classes, own), jnp.bfloat16),
            pltpu.VMEM((ITERS + 1, n, classes, own), jnp.bfloat16),
            pltpu.VMEM((ITERS + 1, rows, classes, width), jnp.float32),
            pltpu.VMEM((dots, 2, 8, LANES), jnp.float32),
            pltpu.VMEM((dots, n, 2, 8, LANES), jnp.float32),
            dma((n,)),
            dma((ITERS + 1, n)), dma((ITERS + 1, n)),
            dma((ITERS + 1, n)), dma((ITERS + 1, n)),
            dma((ITERS + 1, rows)), dma((ITERS + 1, rows)),
            dma((dots, n)), dma((dots, n)),
        ],
        compiler_params=pltpu.CompilerParams(
            collective_id=0, has_side_effects=True, vmem_limit_bytes=40 * 1024 * 1024
        ),
        name="newton_step",
    )(
        covariates.reshape(n, own, width), labels.reshape(n, 1, own), weights, sample_index.reshape(1, sub)
    )


def solution(mesh):
    in_specs = (P("row", "col"), P("row"), P(None, "col"), P("row"))
    out_specs = (P(None, "col"), P(None, "col"))
    return jax.shard_map(body, mesh=mesh, in_specs=in_specs, out_specs=out_specs, check_vma=False)
```

time: 382 us -> 87.9 us (0.23)
  blocking collectives: 166 us -> 0 us
  waiting for transfers between devices: 128 us -> 0 us
  Pallas kernels: 0 us -> 80.1 us
  local copies, waits for them, and re-layouts: 38.1 us -> 6.84 us
  matrix products: 24.2 us -> 0 us
  between operations: 17.9 us -> 0.65 us
  other arithmetic: 6.95 us -> 0 us
    psum x6 -> x0, blocking collectives: 166 us -> none  [the longest x1 40.4 us: body(): norm_new = lax.psum(local_inner(residual, residual), ('row', 'col'))]
    psum x3 -> x0, waiting for transfers between devices: 128 us -> none  [the longest x2 91.3 us: body(): response = lax.psum(partial_response, 'col')]
    pallas_call x0 -> x1, Pallas kernels: none -> 80.1 us  [body(): pl.pallas_call(functools.partial(kernel, n, rows, users * rows, sub * row...]
    gather x3 -> x0, local copies, waits for them, and re-layouts: 35.4 us -> none  [the longest x1 21.8 us: body(): sub_rows = jnp.take(covariates, within, axis=0)]
    dot_general x6 -> x0, matrix products: 24.2 us -> none  [the longest x2 7.46 us: body(): lax.dot_general(rounded, sub_rows, (((1,), (1,)), ((), ())), preferred_el...]
    unnamed x8 -> x10, local copies, waits for them, and re-layouts: 0.02 us -> 6.84 us
    reduce_sum x6 -> x0, other arithmetic: 5.11 us -> none  [the longest x2 2.03 us: body(): centred = response - jnp.sum(sub_shares * response, axis=0, keepdims=True)]
  transfers between devices with their start and end apart: 3 -> 0, of which waited for: 3 -> 0; matrix products, arithmetic and copies ran while one was open for 10% -> 0% of each run, Pallas kernels for 0% -> 0%
where the time goes in v1:
time: 87.9 us; the launch traced here: 87.6 us
  Pallas kernels  80.1 us (91%)
  local copies, waits for them, and re-layouts  6.84 us (8%)
    pallas_call x1, Pallas kernels, body(): pl.pallas_call(functools.partial(kernel, n, rows, users * rows, sub * row...  80.1 us
    unnamed x10, local copies, waits for them, and re-layouts  6.84 us

profile of v1, /device:TPU:0, one launch (start us, length us, event | category | flops | bytes accessed | tf_op | source)
XLA Modules:
  0.0 87.6 jit_solution(11572007260037734255)
XLA Ops:
  0.6 0.0 copy-start
  0.6 3.4 %copy-done = bf16[8192,512]{1,0:T(8,128)(2,1)S(1)} copy-done((bf16[8192,512]{1,0:T(8,128)(2,1)S(1)}, bf16[8192,512]{1,0:T(8,128)(2,1)}, u32[]{:S(2)}) %copy-start) | copy-done | bytes 8388632
  4.0 0.0 copy-start.1
  4.0 0.8 copy-done.1
  4.8 0.0 copy-start.2
  4.8 0.8 copy-done.2
  5.5 0.0 copy-start.3
  5.5 0.7 copy-done.3
  6.2 80.1 %newton_step.1 = (f32[16,512]{1,0:T(8,128)S(1)}, f32[16,512]{1,0:T(8,128)S(1)}) custom-call(bf16[8,1024,512]{2,1,0:T(8,128)(2,1)S(1)} %bitcast.3, s32[8,1,1024]{2,1,0:T(1,128)S(1)} %bitcast.4, f32[16,512]{1,0:T(8,128)S(1)} %copy-done.2, s32[1,4096]{1,0:T(1,128)S(1)} %bitcast.5), custom_call_target="tpu_custom_call" | custom-call | tf_op jit(solution)/shard_map/newton_step/pallas_call | solution.py:247
  86.4 0.6 copy.8
  87.0 0.6 copy.9
Async XLA Ops:
  0.6 3.4 %copy-start = (bf16[8192,512]{1,0:T(8,128)(2,1)S(1)}, bf16[8192,512]{1,0:T(8,128)(2,1)}, u32[]{:S(2)}) copy-start(bf16[8192,512]{1,0:T(8,128)(2,1)} %param.4) | copy-start | bytes 25165828
  4.0 0.8 copy-start.1
  4.8 0.8 copy-start.2
  5.5 0.7 copy-start.3

commit v2 on v1

--- a/solution.py
+++ b/solution.py
@@ -23,9 +23,11 @@
 
 def kernel(
     n, rows, user_total, sub_total,
-    cov_hbm, labels_ref, weights_ref, index_ref, gradient_ref, step_ref,
-    cov, logit_send, logit_recv, resp_send, resp_recv, share_send, share_recv, row_buf, dot_send, dot_recv,
-    cov_sem, rs_ssem, rs_rsem, ag_ssem, ag_rsem, row_ssem, row_rsem, dot_ssem, dot_rsem,
+    cov_hbm, labels_hbm, weights_hbm, index_hbm, gradient_ref, step_ref,
+    cov, labels_ref, weights_ref, index_ref, pair_send, pair_recv, logit_send, logit_recv, resp_send, resp_recv,
+    share_send, share_recv, pass_recv, row_buf, dot_send, dot_recv,
+    cov_sem, small_sem, pair_ssem, pair_rsem, rs_ssem, rs_rsem, ag_ssem, ag_rsem, pass_ssem, pass_rsem,
+    row_ssem, row_rsem, dot_ssem, dot_rsem,
 ):
     me = lax.axis_index("col")
     my_row = lax.axis_index("row")
@@ -33,21 +35,42 @@
     own = cov.shape[1]
     classes = weights_ref.shape[0]
 
+    chip, core = me // 2, lax.rem(me, 2)
+    sibling = chip * 2 + 1 - core
+
     def target(j):
-        return lax.rem(me // 2 + j // 2, chips) * 2 + lax.rem(lax.rem(me, 2) + lax.rem(j, 2), 2)
-
-    def source(j):
-        return lax.rem(me // 2 + chips - j // 2, chips) * 2 + lax.rem(lax.rem(me, 2) + 2 - lax.rem(j, 2), 2)
-
-    def cov_copy(j):
-        block = target(j)
-        return pltpu.make_async_copy(cov_hbm.at[block], cov.at[block], cov_sem.at[j])
+        return lax.rem(me + j, n)
+
+    def chip_after(s):
+        return lax.rem(chip + s, chips)
+
+    def chip_before(s):
+        return lax.rem(chip + chips - s, chips)
+
+    def theirs(i):
+        return chip_after(chips - 1 - i) * 2 + 1 - core
+
+    def mine(i):
+        return chip_after(chips - 1 - i) * 2 + core
+
+    def cov_copy(side, i):
+        block = theirs(i) if side == 0 else mine(i)
+        return pltpu.make_async_copy(cov_hbm.at[block], cov.at[block], cov_sem.at[side, i])
+
+    small_copies = [
+        pltpu.make_async_copy(weights_hbm, weights_ref, small_sem.at[0]),
+        pltpu.make_async_copy(index_hbm, index_ref, small_sem.at[1]),
+        pltpu.make_async_copy(labels_hbm.at[me], labels_ref, small_sem.at[2]),
+    ]
+    for copy in small_copies:
+        copy.start()
 
     def start_cov(i, carry):
-        cov_copy(n - 1 - i).start()
-        return carry
-
-    lax.fori_loop(0, n, start_cov, 0)
+        cov_copy(0, i).start()
+        cov_copy(1, i).start()
+        return carry
+
+    lax.fori_loop(0, chips, start_cov, 0)
 
     barrier = pltpu.get_barrier_semaphore()
 
@@ -63,6 +86,9 @@
 
     lax.fori_loop(1, n, greet_col, 0)
     lax.fori_loop(1, rows, greet_row, 0)
+
+    for copy in small_copies:
+        copy.wait()
 
     groups = own // LANES
     padded = max(16, groups)
@@ -79,11 +105,18 @@
 
     pl.semaphore_wait(barrier, n - 1 + rows - 1)
 
-    def rs_copy(phase, send, recv, j):
-        return pltpu.make_async_remote_copy(
-            src_ref=send.at[j], dst_ref=recv.at[j],
-            send_sem=rs_ssem.at[phase, j], recv_sem=rs_rsem.at[phase, j],
-            device_id={"col": target(j)}, device_id_type=MESH,
+    def pair_copy(phase, i):
+        return pltpu.make_async_remote_copy(
+            src_ref=pair_send.at[phase, i], dst_ref=pair_recv.at[phase, i],
+            send_sem=pair_ssem.at[phase, i], recv_sem=pair_rsem.at[phase, i],
+            device_id={"col": sibling}, device_id_type=MESH,
+        )
+
+    def rs_copy(phase, send, recv, i):
+        return pltpu.make_async_remote_copy(
+            src_ref=send.at[i], dst_ref=recv.at[i],
+            send_sem=rs_ssem.at[phase, i], recv_sem=rs_rsem.at[phase, i],
+            device_id={"col": mine(i)}, device_id_type=MESH,
         )
 
     def project(vector, block):
@@ -92,29 +125,53 @@
         )
 
     def reduce_users(phase, vector, send, recv):
-        def one(i, carry):
-            j = n - 1 - i
+        def for_sibling(i):
             if phase == 0:
-                cov_copy(j).wait()
-            send[j] = project(vector, target(j)).astype(send.dtype)
-            rs_copy(phase, send, recv, j).start()
-            return carry
-
-        lax.fori_loop(0, n - 1, one, 0)
-        if phase == 0:
-            cov_copy(0).wait()
-
-        def add(j, total):
-            rs_copy(phase, send, recv, j).wait_recv()
-            return total + recv[j].astype(jnp.float32)
-
-        return lax.fori_loop(1, n, add, project(vector, me))
-
-    def ag_copy(phase, j):
-        return pltpu.make_async_remote_copy(
-            src_ref=share_send.at[phase], dst_ref=share_recv.at[phase, j],
-            send_sem=ag_ssem.at[phase, j], recv_sem=ag_rsem.at[phase, j],
-            device_id={"col": target(j)}, device_id_type=MESH,
+                cov_copy(0, i).wait()
+            pair_send[phase, i] = project(vector, theirs(i))
+            pair_copy(phase, i).start()
+
+        def for_own(i):
+            if phase == 0:
+                cov_copy(1, i).wait()
+            part = project(vector, mine(i))
+            pair_copy(phase, i).wait_recv()
+            return part + pair_recv[phase, i]
+
+        def send_own(i):
+            send[i] = for_own(i).astype(send.dtype)
+            rs_copy(phase, send, recv, i).start()
+
+        def both(i, carry):
+            send_own(i)
+            for_sibling(i + 2)
+            return carry
+
+        for_sibling(0)
+        for_sibling(1)
+        lax.fori_loop(0, chips - 2, both, 0)
+        send_own(chips - 2)
+
+        def add(i, total):
+            rs_copy(phase, send, recv, i).wait_recv()
+            return total + recv[i].astype(jnp.float32)
+
+        return lax.fori_loop(0, chips - 1, add, for_own(chips - 1))
+
+    def ag_copy(phase, s):
+        peer = sibling if s is None else chip_after(s) * 2 + core
+        slot = 0 if s is None else s
+        return pltpu.make_async_remote_copy(
+            src_ref=share_send.at[phase], dst_ref=share_recv.at[phase, slot],
+            send_sem=ag_ssem.at[phase, slot], recv_sem=ag_rsem.at[phase, slot],
+            device_id={"col": peer}, device_id_type=MESH,
+        )
+
+    def forward(phase, s):
+        return pltpu.make_async_remote_copy(
+            src_ref=share_recv.at[phase, s], dst_ref=pass_recv.at[phase, s],
+            send_sem=pass_ssem.at[phase, s], recv_sem=pass_rsem.at[phase, s],
+            device_id={"col": sibling}, device_id_type=MESH,
         )
 
     def row_copy(phase, t, slot):
@@ -127,21 +184,34 @@
     def back_project(phase, values):
         share_send[phase] = values
 
-        def send(j, carry):
-            ag_copy(phase, j).start()
-            return carry
-
-        lax.fori_loop(1, n, send, 0)
-
-        def add(j, total):
-            ag_copy(phase, j).wait_recv()
-            return total + jnp.dot(
-                share_recv[phase, j], cov[source(j)], preferred_element_type=jnp.float32
-            )
-
-        row_buf[phase, my_row] = lax.fori_loop(
-            1, n, add, jnp.dot(values, cov[me], preferred_element_type=jnp.float32)
-        )
+        ag_copy(phase, None).start()
+
+        def send(s, carry):
+            ag_copy(phase, s).start()
+            return carry
+
+        lax.fori_loop(1, chips, send, 0)
+
+        def term(block_values, block):
+            return jnp.dot(block_values, cov[block], preferred_element_type=jnp.float32)
+
+        def direct(s):
+            ag_copy(phase, s).wait_recv()
+            forward(phase, s).start()
+            return term(share_recv[phase, s], chip_before(s) * 2 + core)
+
+        def passed(s):
+            forward(phase, s).wait_recv()
+            return term(pass_recv[phase, s], chip_before(s) * 2 + 1 - core)
+
+        def both(s, total):
+            return total + direct(s + 1) + passed(s)
+
+        total = term(values, me)
+        ag_copy(phase, None).wait_recv()
+        total = total + term(share_recv[phase, 0], sibling) + direct(1)
+        total = lax.fori_loop(1, chips - 1, both, total)
+        row_buf[phase, my_row] = total + passed(chips - 1)
 
         def send_row(t, carry):
             row_copy(phase, t, my_row).start()
@@ -185,7 +255,7 @@
     logits = reduce_users(0, weights.astype(jnp.bfloat16), logit_send, logit_recv)
     exponent = jnp.exp(logits)
     shares = exponent / jnp.sum(exponent, axis=0, keepdims=True)
-    label = labels_ref[me]
+    label = labels_ref[...]
     indicator = (label == lax.broadcasted_iota(jnp.int32, (classes, own), 0)).astype(jnp.float32)
     misfit = (shares - indicator).astype(jnp.bfloat16)
     gradient = back_project(0, misfit) / user_total + RIDGE_WEIGHT * weights
@@ -216,12 +286,21 @@
             norm_now = norm_new
     step_ref[...] = newton_step
 
+    def drain_pair(i, carry):
+        for phase in range(ITERS + 1):
+            pair_copy(phase, i).wait_send()
+        return carry
+
+    def drain_chip(s, carry):
+        rs_copy(0, logit_send, logit_recv, s - 1).wait_send()
+        for phase in range(ITERS):
+            rs_copy(phase + 1, resp_send.at[phase], resp_recv.at[phase], s - 1).wait_send()
+        for phase in range(ITERS + 1):
+            ag_copy(phase, s).wait_send()
+            forward(phase, s).wait_send()
+        return carry
+
     def drain_col(j, carry):
-        rs_copy(0, logit_send, logit_recv, j).wait_send()
-        for phase in range(ITERS):
-            rs_copy(phase + 1, resp_send.at[phase], resp_recv.at[phase], j).wait_send()
-        for phase in range(ITERS + 1):
-            ag_copy(phase, j).wait_send()
         for phase in range(2 * ITERS - 1):
             dot_copy(phase, j).wait_send()
         return carry
@@ -231,6 +310,10 @@
             row_copy(phase, t, my_row).wait_send()
         return carry
 
+    for phase in range(ITERS + 1):
+        ag_copy(phase, None).wait_send()
+    lax.fori_loop(0, chips, drain_pair, 0)
+    lax.fori_loop(1, chips, drain_chip, 0)
     lax.fori_loop(1, n, drain_col, 0)
     lax.fori_loop(1, rows, drain_row, 0)
 
@@ -238,7 +321,7 @@
 def body(covariates, labels, weights, sample_index):
     users, width = covariates.shape
     n, rows = lax.axis_size("col"), lax.axis_size("row")
-    own = users // n
+    own, chips = users // n, n // 2
     classes = weights.shape[0]
     sub = sample_index.shape[0]
     dots = 2 * ITERS - 1
@@ -247,22 +330,30 @@
     return pl.pallas_call(
         functools.partial(kernel, n, rows, users * rows, sub * rows),
         out_shape=[jax.ShapeDtypeStruct((classes, width), jnp.float32)] * 2,
-        in_specs=[pl.BlockSpec(memory_space=pl.ANY), vmem, vmem, vmem],
+        in_specs=[pl.BlockSpec(memory_space=pltpu.HBM)] * 4,
         out_specs=[vmem, vmem],
         scratch_shapes=[
             pltpu.VMEM((n, own, width), jnp.bfloat16),
-            pltpu.VMEM((n, classes, own), jnp.float32),
-            pltpu.VMEM((n, classes, own), jnp.float32),
-            pltpu.VMEM((ITERS, n, classes, own), jnp.bfloat16),
-            pltpu.VMEM((ITERS, n, classes, own), jnp.bfloat16),
+            pltpu.VMEM((1, own), jnp.int32),
+            pltpu.VMEM((classes, width), jnp.float32),
+            pltpu.VMEM((1, sub), jnp.int32),
+            pltpu.VMEM((ITERS + 1, chips, classes, own), jnp.float32),
+            pltpu.VMEM((ITERS + 1, chips, classes, own), jnp.float32),
+            pltpu.VMEM((chips, classes, own), jnp.float32),
+            pltpu.VMEM((chips, classes, own), jnp.float32),
+            pltpu.VMEM((ITERS, chips, classes, own), jnp.bfloat16),
+            pltpu.VMEM((ITERS, chips, classes, own), jnp.bfloat16),
             pltpu.VMEM((ITERS + 1, classes, own), jnp.bfloat16),
-            pltpu.VMEM((ITERS + 1, n, classes, own), jnp.bfloat16),
+            pltpu.VMEM((ITERS + 1, chips, classes, own), jnp.bfloat16),
+            pltpu.VMEM((ITERS + 1, chips, classes, own), jnp.bfloat16),
             pltpu.VMEM((ITERS + 1, rows, classes, width), jnp.float32),
             pltpu.VMEM((dots, 2, 8, LANES), jnp.float32),
             pltpu.VMEM((dots, n, 2, 8, LANES), jnp.float32),
-            dma((n,)),
-            dma((ITERS + 1, n)), dma((ITERS + 1, n)),
-            dma((ITERS + 1, n)), dma((ITERS + 1, n)),
+            dma((2, chips)), dma((3,)),
+            dma((ITERS + 1, chips)), dma((ITERS + 1, chips)),
+            dma((ITERS + 1, chips)), dma((ITERS + 1, chips)),
+            dma((ITERS + 1, chips)), dma((ITERS + 1, chips)),
+            dma((ITERS + 1, chips)), dma((ITERS + 1, chips)),
             dma((ITERS + 1, rows)), dma((ITERS + 1, rows)),
             dma((dots, n)), dma((dots, n)),
         ],

time: 87.9 us -> 81.2 us (0.924)
  Pallas kernels: 80.1 us -> 73.4 us
    pallas_call x1, Pallas kernels: 80.1 us -> 73.4 us  [body(): pl.pallas_call(functools.partial(kernel, n, rows, users * rows, sub * row...]
where the time goes in v2:
time: 81.2 us; the launch traced here: 80.9 us
  Pallas kernels  73.4 us (90%)
  local copies, waits for them, and re-layouts  6.84 us (8%)
    pallas_call x1, Pallas kernels, body(): pl.pallas_call(functools.partial(kernel, n, rows, users * rows, sub * row...  73.4 us
    unnamed x10, local copies, waits for them, and re-layouts  6.84 us

profile of v2, /device:TPU:0, one launch (start us, length us, event | category | flops | bytes accessed | tf_op | source)
XLA Modules:
  0.0 80.9 jit_solution(5289908356516084955)
XLA Ops:
  0.6 0.0 copy-start
  0.6 3.4 %copy-done = bf16[8192,512]{1,0:T(8,128)(2,1)S(1)} copy-done((bf16[8192,512]{1,0:T(8,128)(2,1)S(1)}, bf16[8192,512]{1,0:T(8,128)(2,1)}, u32[]{:S(2)}) %copy-start) | copy-done | bytes 8388632
  4.0 0.0 copy-start.1
  4.0 0.8 copy-done.1
  4.8 0.0 copy-start.2
  4.8 0.8 copy-done.2
  5.5 0.0 copy-start.3
  5.5 0.7 copy-done.3
  6.2 73.4 %newton_step.1 = (f32[16,512]{1,0:T(8,128)S(1)}, f32[16,512]{1,0:T(8,128)S(1)}) custom-call(bf16[8,1024,512]{2,1,0:T(8,128)(2,1)S(1)} %bitcast.3, s32[8,1,1024]{2,1,0:T(1,128)S(1)} %bitcast.4, f32[16,512]{1,0:T(8,128)S(1)} %copy-done.2, s32[1,4096]{1,0:T(1,128)S(1)} %bitcast.5), custom_call_target="tpu_custom_call" | custom-call | tf_op jit(solution)/shard_map/newton_step/pallas_call | solution.py:330
  79.6 0.6 copy.8
  80.3 0.6 copy.9
Async XLA Ops:
  0.6 3.4 %copy-start = (bf16[8192,512]{1,0:T(8,128)(2,1)S(1)}, bf16[8192,512]{1,0:T(8,128)(2,1)}, u32[]{:S(2)}) copy-start(bf16[8192,512]{1,0:T(8,128)(2,1)} %param.4) | copy-start | bytes 25165828
  4.0 0.8 copy-start.1
  4.8 0.8 copy-start.2
  5.5 0.7 copy-start.3

commit v3 on v2

--- a/solution.py
+++ b/solution.py
@@ -23,11 +23,11 @@
 
 def kernel(
     n, rows, user_total, sub_total,
-    cov_hbm, labels_hbm, weights_hbm, index_hbm, gradient_ref, step_ref,
+    cov_hbm, labels_hbm, weights_hbm, index_hbm, out_ref,
     cov, labels_ref, weights_ref, index_ref, pair_send, pair_recv, logit_send, logit_recv, resp_send, resp_recv,
-    share_send, share_recv, pass_recv, row_buf, dot_send, dot_recv,
+    share_send, share_recv, pass_recv, row_buf, curve_buf, dot_send, dot_recv,
     cov_sem, small_sem, pair_ssem, pair_rsem, rs_ssem, rs_rsem, ag_ssem, ag_rsem, pass_ssem, pass_rsem,
-    row_ssem, row_rsem, dot_ssem, dot_rsem,
+    row_ssem, row_rsem, curve_ssem, curve_rsem, dot_ssem, dot_rsem,
 ):
     me = lax.axis_index("col")
     my_row = lax.axis_index("row")
@@ -181,7 +181,7 @@
             device_id={"row": lax.rem(my_row + t, rows)}, device_id_type=MESH,
         )
 
-    def back_project(phase, values):
+    def back_project(phase, values, meanwhile=None):
         share_send[phase] = values
 
         ag_copy(phase, None).start()
@@ -211,6 +211,8 @@
         ag_copy(phase, None).wait_recv()
         total = total + term(share_recv[phase, 0], sibling) + direct(1)
         total = lax.fori_loop(1, chips - 1, both, total)
+        if meanwhile is not None:
+            meanwhile()
         row_buf[phase, my_row] = total + passed(chips - 1)
 
         def send_row(t, carry):
@@ -235,21 +237,50 @@
             device_id={"col": target(j)}, device_id_type=MESH,
         )
 
-    def inner(phase, *pairs):
-        for k, (first, second) in enumerate(pairs):
-            dot_send[phase, k] = fold(first * second)
+    def send_dots(phase, *tiles):
+        for k, tile in enumerate(tiles):
+            dot_send[phase, k] = tile
 
         def send(j, carry):
             dot_copy(phase, j).start()
             return carry
 
+        lax.fori_loop(1, n, send, 0)
+
+    def take_dots(phase, tiles):
         def add(j, totals):
             dot_copy(phase, j).wait_recv()
             return tuple(total + dot_recv[phase, j, k] for k, total in enumerate(totals))
 
-        lax.fori_loop(1, n, send, 0)
-        totals = lax.fori_loop(1, n, add, tuple(dot_send[phase, k] for k in range(len(pairs))))
+        totals = lax.fori_loop(1, n, add, tuple(dot_send[phase, k] for k in range(tiles)))
         return [jnp.sum(total, keepdims=True) for total in totals]
+
+    def curve_copy(phase, t, slot):
+        return pltpu.make_async_remote_copy(
+            src_ref=curve_buf.at[phase, my_row], dst_ref=curve_buf.at[phase, slot],
+            send_sem=curve_ssem.at[phase, t], recv_sem=curve_rsem.at[phase, t],
+            device_id={"row": lax.rem(my_row + t, rows)}, device_id_type=MESH,
+        )
+
+    def send_curve(phase, tile):
+        curve_buf[phase, my_row] = tile
+
+        def send(t, carry):
+            curve_copy(phase, t, my_row).start()
+            return carry
+
+        lax.fori_loop(1, rows, send, 0)
+
+    def take_curve(phase):
+        def wait(t, carry):
+            curve_copy(phase, t, lax.rem(my_row + rows - t, rows)).wait_recv()
+            return carry
+
+        lax.fori_loop(1, rows, wait, 0)
+        total = curve_buf[phase, 0]
+        for r in range(1, rows):
+            total = total + curve_buf[phase, r]
+        return total
 
     weights = weights_ref[...]
     logits = reduce_users(0, weights.astype(jnp.bfloat16), logit_send, logit_recv)
@@ -259,32 +290,51 @@
     indicator = (label == lax.broadcasted_iota(jnp.int32, (classes, own), 0)).astype(jnp.float32)
     misfit = (shares - indicator).astype(jnp.bfloat16)
     gradient = back_project(0, misfit) / user_total + RIDGE_WEIGHT * weights
-    gradient_ref[...] = gradient
+    out_ref[0] = gradient
     counted = count * shares
 
     residual = -gradient
     direction = residual
     newton_step = jnp.zeros_like(residual)
-    norm_now = None
+    norm_now = step_size = image = residual_response = direction_response = None
     for iteration in range(ITERS):
+        last = iteration + 1 == ITERS
+        vector = direction if iteration == 0 else image
         response = reduce_users(
-            iteration + 1, direction.astype(jnp.bfloat16), resp_send.at[iteration], resp_recv.at[iteration]
-        )
-        centred = response - jnp.sum(shares * response, axis=0, keepdims=True)
+            iteration + 1, vector.astype(jnp.bfloat16), resp_send.at[iteration], resp_recv.at[iteration]
+        )
+        if iteration == 0:
+            residual_response = direction_response = response
+        else:
+            (norm_new,) = take_dots(2 * iteration - 1, 1)
+            ratio = norm_new / norm_now
+            direction = residual + ratio * direction
+            norm_now = norm_new
+            residual_response = residual_response - step_size * response
+            direction_response = residual_response + ratio * direction_response
+        centred = direction_response - jnp.sum(shares * direction_response, axis=0, keepdims=True)
         weighted = (counted * centred).astype(jnp.bfloat16)
-        image = back_project(iteration + 1, weighted) / sub_total + RIDGE_WEIGHT * direction
-        if norm_now is None:
-            curve, norm_now = inner(2 * iteration, (direction, image), (residual, residual))
+        send_curve(iteration, fold(weighted.astype(jnp.float32) * direction_response))
+        square = fold(direction * direction)
+
+        def pass_curve():
+            tiles = [take_curve(iteration) / sub_total + RIDGE_WEIGHT * square]
+            send_dots(2 * iteration, *(tiles + [square] if iteration == 0 else tiles))
+
+        if last:
+            pass_curve()
         else:
-            (curve,) = inner(2 * iteration, (direction, image))
+            image = back_project(iteration + 1, weighted, pass_curve) / sub_total + RIDGE_WEIGHT * direction
+        if iteration == 0:
+            curve, norm_now = take_dots(0, 2)
+        else:
+            (curve,) = take_dots(2 * iteration, 1)
         step_size = norm_now / curve
         newton_step = newton_step + step_size * direction
-        residual = residual - step_size * image
-        if iteration + 1 < ITERS:
-            (norm_new,) = inner(2 * iteration + 1, (residual, residual))
-            direction = residual + (norm_new / norm_now) * direction
-            norm_now = norm_new
-    step_ref[...] = newton_step
+        if not last:
+            residual = residual - step_size * image
+            send_dots(2 * iteration + 1, fold(residual * residual))
+    out_ref[1] = newton_step
 
     def drain_pair(i, carry):
         for phase in range(ITERS + 1):
@@ -295,7 +345,7 @@
         rs_copy(0, logit_send, logit_recv, s - 1).wait_send()
         for phase in range(ITERS):
             rs_copy(phase + 1, resp_send.at[phase], resp_recv.at[phase], s - 1).wait_send()
-        for phase in range(ITERS + 1):
+        for phase in range(ITERS):
             ag_copy(phase, s).wait_send()
             forward(phase, s).wait_send()
         return carry
@@ -306,11 +356,12 @@
         return carry
 
     def drain_row(t, carry):
-        for phase in range(ITERS + 1):
+        for phase in range(ITERS):
             row_copy(phase, t, my_row).wait_send()
-        return carry
-
-    for phase in range(ITERS + 1):
+            curve_copy(phase, t, my_row).wait_send()
+        return carry
+
+    for phase in range(ITERS):
         ag_copy(phase, None).wait_send()
     lax.fori_loop(0, chips, drain_pair, 0)
     lax.fori_loop(1, chips, drain_chip, 0)
@@ -326,12 +377,11 @@
     sub = sample_index.shape[0]
     dots = 2 * ITERS - 1
     dma = pltpu.SemaphoreType.DMA
-    vmem = pl.BlockSpec(memory_space=pltpu.VMEM)
-    return pl.pallas_call(
+    out = pl.pallas_call(
         functools.partial(kernel, n, rows, users * rows, sub * rows),
-        out_shape=[jax.ShapeDtypeStruct((classes, width), jnp.float32)] * 2,
+        out_shape=jax.ShapeDtypeStruct((2, classes, width), jnp.float32),
         in_specs=[pl.BlockSpec(memory_space=pltpu.HBM)] * 4,
-        out_specs=[vmem, vmem],
+        out_specs=pl.BlockSpec(memory_space=pltpu.VMEM),
         scratch_shapes=[
             pltpu.VMEM((n, own, width), jnp.bfloat16),
             pltpu.VMEM((1, own), jnp.int32),
@@ -343,27 +393,30 @@
             pltpu.VMEM((chips, classes, own), jnp.float32),
             pltpu.VMEM((ITERS, chips, classes, own), jnp.bfloat16),
             pltpu.VMEM((ITERS, chips, classes, own), jnp.bfloat16),
-            pltpu.VMEM((ITERS + 1, classes, own), jnp.bfloat16),
-            pltpu.VMEM((ITERS + 1, chips, classes, own), jnp.bfloat16),
-            pltpu.VMEM((ITERS + 1, chips, classes, own), jnp.bfloat16),
-            pltpu.VMEM((ITERS + 1, rows, classes, width), jnp.float32),
+            pltpu.VMEM((ITERS, classes, own), jnp.bfloat16),
+            pltpu.VMEM((ITERS, chips, classes, own), jnp.bfloat16),
+            pltpu.VMEM((ITERS, chips, classes, own), jnp.bfloat16),
+            pltpu.VMEM((ITERS, rows, classes, width), jnp.float32),
+            pltpu.VMEM((ITERS, rows, 8, LANES), jnp.float32),
             pltpu.VMEM((dots, 2, 8, LANES), jnp.float32),
             pltpu.VMEM((dots, n, 2, 8, LANES), jnp.float32),
             dma((2, chips)), dma((3,)),
             dma((ITERS + 1, chips)), dma((ITERS + 1, chips)),
             dma((ITERS + 1, chips)), dma((ITERS + 1, chips)),
-            dma((ITERS + 1, chips)), dma((ITERS + 1, chips)),
-            dma((ITERS + 1, chips)), dma((ITERS + 1, chips)),
-            dma((ITERS + 1, rows)), dma((ITERS + 1, rows)),
+            dma((ITERS, chips)), dma((ITERS, chips)),
+            dma((ITERS, chips)), dma((ITERS, chips)),
+            dma((ITERS, rows)), dma((ITERS, rows)),
+            dma((ITERS, rows)), dma((ITERS, rows)),
             dma((dots, n)), dma((dots, n)),
         ],
         compiler_params=pltpu.CompilerParams(
-            collective_id=0, has_side_effects=True, vmem_limit_bytes=40 * 1024 * 1024
+            collective_id=0, has_side_effects=True, vmem_limit_bytes=60 * 1024 * 1024
         ),
         name="newton_step",
     )(
         covariates.reshape(n, own, width), labels.reshape(n, 1, own), weights, sample_index.reshape(1, sub)
     )
+    return out[0], out[1]
 
 
 def solution(mesh):

time: 81.2 us -> 61.5 us (0.76)
  Pallas kernels: 73.4 us -> 59.3 us
  local copies, waits for them, and re-layouts: 6.84 us -> 1.41 us
    pallas_call x1, Pallas kernels: 73.4 us -> 59.3 us  [body(): pl.pallas_call(functools.partial(kernel, n, rows, users * rows, sub * row...]
    unnamed x10 -> x0, local copies, waits for them, and re-layouts: 6.84 us -> none
    squeeze x0 -> x1, local copies, waits for them, and re-layouts: none -> 1.41 us  [body(): return (out[0], out[1])]
where the time goes in v3:
time: 61.5 us; the launch traced here: 61.3 us
  Pallas kernels  59.3 us (96%)
  local copies, waits for them, and re-layouts  1.41 us (2%)
  between operations  0.64 us (1%)
    pallas_call x1, Pallas kernels, body(): pl.pallas_call(functools.partial(kernel, n, rows, users * rows, sub * row...  59.3 us
    squeeze x1, local copies, waits for them, and re-layouts, body(): return (out[0], out[1])  1.41 us

profile of v3, /device:TPU:0, one launch (start us, length us, event | category | flops | bytes accessed | tf_op | source)
XLA Modules:
  0.0 61.3 jit_solution(5170247773044098550)
XLA Ops:
  0.6 59.3 %newton_step.1 = f32[2,16,512]{2,1,0:T(8,128)} custom-call(bf16[8,1024,512]{2,1,0:T(8,128)(2,1)} %bitcast.7, s32[8,1,1024]{2,1,0:T(1,128)} %bitcast.8, f32[16,512]{1,0:T(8,128)} %weights_hbm.1, s32[1,4096]{1,0:T(1,128)} %bitcast.9), custom_call_target="tpu_custom_call" | custom-call | tf_op jit(solution)/shard_map/newton_step/pallas_call | solution.py:380
  59.9 1.4 %slice_bitcast_fusion = (f32[16,512]{1,0:T(8,128)}, f32[16,512]{1,0:T(8,128)}) fusion(f32[2,16,512]{2,1,0:T(8,128)} %newton_step.1), kind=kLoop, calls=%fused_computation | loop fusion | bytes 131072 | tf_op jit(solution)/shard_map/squeeze | solution.py:419

commit v4 on v3

--- a/solution.py
+++ b/solution.py
@@ -23,7 +23,7 @@
 
 def kernel(
     n, rows, user_total, sub_total,
-    cov_hbm, labels_hbm, weights_hbm, index_hbm, out_ref,
+    cov_hbm, labels_hbm, weights_hbm, index_hbm, gradient_ref, step_ref,
     cov, labels_ref, weights_ref, index_ref, pair_send, pair_recv, logit_send, logit_recv, resp_send, resp_recv,
     share_send, share_recv, pass_recv, row_buf, curve_buf, dot_send, dot_recv,
     cov_sem, small_sem, pair_ssem, pair_rsem, rs_ssem, rs_rsem, ag_ssem, ag_rsem, pass_ssem, pass_rsem,
@@ -120,11 +120,11 @@
         )
 
     def project(vector, block):
-        return lax.dot_general(
-            vector, cov[block], (((1,), (1,)), ((), ())), preferred_element_type=jnp.float32
-        )
+        return jnp.dot(cov[block], vector, preferred_element_type=jnp.float32).T
 
     def reduce_users(phase, vector, send, recv):
+        vector = vector.T.astype(jnp.bfloat16)
+
         def for_sibling(i):
             if phase == 0:
                 cov_copy(0, i).wait()
@@ -283,14 +283,14 @@
         return total
 
     weights = weights_ref[...]
-    logits = reduce_users(0, weights.astype(jnp.bfloat16), logit_send, logit_recv)
+    logits = reduce_users(0, weights, logit_send, logit_recv)
     exponent = jnp.exp(logits)
     shares = exponent / jnp.sum(exponent, axis=0, keepdims=True)
     label = labels_ref[...]
     indicator = (label == lax.broadcasted_iota(jnp.int32, (classes, own), 0)).astype(jnp.float32)
     misfit = (shares - indicator).astype(jnp.bfloat16)
     gradient = back_project(0, misfit) / user_total + RIDGE_WEIGHT * weights
-    out_ref[0] = gradient
+    gradient_ref[...] = gradient
     counted = count * shares
 
     residual = -gradient
@@ -301,7 +301,7 @@
         last = iteration + 1 == ITERS
         vector = direction if iteration == 0 else image
         response = reduce_users(
-            iteration + 1, vector.astype(jnp.bfloat16), resp_send.at[iteration], resp_recv.at[iteration]
+            iteration + 1, vector, resp_send.at[iteration], resp_recv.at[iteration]
         )
         if iteration == 0:
             residual_response = direction_response = response
@@ -334,7 +334,7 @@
         if not last:
             residual = residual - step_size * image
             send_dots(2 * iteration + 1, fold(residual * residual))
-    out_ref[1] = newton_step
+    step_ref[...] = newton_step
 
     def drain_pair(i, carry):
         for phase in range(ITERS + 1):
@@ -379,9 +379,9 @@
     dma = pltpu.SemaphoreType.DMA
     out = pl.pallas_call(
         functools.partial(kernel, n, rows, users * rows, sub * rows),
-        out_shape=jax.ShapeDtypeStruct((2, classes, width), jnp.float32),
+        out_shape=[jax.ShapeDtypeStruct((classes, width), jnp.float32)] * 2,
         in_specs=[pl.BlockSpec(memory_space=pltpu.HBM)] * 4,
-        out_specs=pl.BlockSpec(memory_space=pltpu.VMEM),
+        out_specs=[pl.BlockSpec(memory_space=pltpu.VMEM)] * 2,
         scratch_shapes=[
             pltpu.VMEM((n, own, width), jnp.bfloat16),
             pltpu.VMEM((1, own), jnp.int32),
@@ -416,7 +416,7 @@
     )(
         covariates.reshape(n, own, width), labels.reshape(n, 1, own), weights, sample_index.reshape(1, sub)
     )
-    return out[0], out[1]
+    return tuple(out)
 
 
 def solution(mesh):

time: 61.5 us -> 64.6 us (1.050)
  Pallas kernels: 59.3 us -> 61 us
  local copies, waits for them, and re-layouts: 1.41 us -> 2.75 us
    unnamed x0 -> x2, local copies, waits for them, and re-layouts: none -> 2.75 us
    pallas_call x1, Pallas kernels: 59.3 us -> 61 us  [body(): pl.pallas_call(functools.partial(kernel, n, rows, users * rows, sub * row...]
    squeeze x1 -> x0, local copies, waits for them, and re-layouts: 1.41 us -> none  [body(): return (out[0], out[1])]
where the time goes in v4:
time: 64.6 us; the launch traced here: 64.4 us
  Pallas kernels  61 us (94%)
  local copies, waits for them, and re-layouts  2.75 us (4%)
    pallas_call x1, Pallas kernels, body(): pl.pallas_call(functools.partial(kernel, n, rows, users * rows, sub * row...  61 us
    unnamed x2, local copies, waits for them, and re-layouts  2.75 us

profile of v4, /device:TPU:0, one launch (start us, length us, event | category | flops | bytes accessed | tf_op | source)
XLA Modules:
  0.0 64.4 jit_solution(13897800030357463189)
XLA Ops:
  0.6 61.0 %newton_step.1 = (f32[16,512]{1,0:T(8,128)}, f32[16,512]{1,0:T(8,128)}) custom-call(bf16[8,1024,512]{2,1,0:T(8,128)(2,1)} %bitcast.3, s32[8,1,1024]{2,1,0:T(1,128)} %bitcast.4, f32[16,512]{1,0:T(8,128)} %weights_hbm.1, s32[1,4096]{1,0:T(1,128)} %bitcast.5), custom_call_target="tpu_custom_call" | custom-call | tf_op jit(solution)/shard_map/newton_step/pallas_call | solution.py:380
  61.6 1.4 %copy.8 = f32[16,512]{1,0:T(8,128)} copy(f32[16,512]{1,0:T(8,128)} %get-tuple-element.4) | data formatting | bytes 65536
  63.0 1.4 %copy.9 = f32[16,512]{1,0:T(8,128)} copy(f32[16,512]{1,0:T(8,128)} %get-tuple-element.5) | data formatting | bytes 65536

commit v5 on v4

--- a/solution.py
+++ b/solution.py
@@ -10,6 +10,7 @@
 ITERS = 2
 RIDGE_WEIGHT = 0.004
 LANES = 128
+UNROLL = 8
 MESH = pl.DeviceIdType.MESH
 
 
@@ -19,6 +20,14 @@
     for start in range(LANES, value.shape[1], LANES):
         total = total + value[:, start:start + LANES]
     return total
+
+
+def loop(first, end, step, carry):
+    if end - first > UNROLL:
+        return lax.fori_loop(first, end, step, carry)
+    for i in range(first, end):
+        carry = step(i, carry)
+    return carry
 
 
 def kernel(
@@ -70,7 +79,7 @@
         cov_copy(1, i).start()
         return carry
 
-    lax.fori_loop(0, chips, start_cov, 0)
+    loop(0, chips, start_cov, 0)
 
     barrier = pltpu.get_barrier_semaphore()
 
@@ -84,8 +93,8 @@
         )
         return carry
 
-    lax.fori_loop(1, n, greet_col, 0)
-    lax.fori_loop(1, rows, greet_row, 0)
+    loop(1, n, greet_col, 0)
+    loop(1, rows, greet_row, 0)
 
     for copy in small_copies:
         copy.wait()
@@ -120,10 +129,12 @@
         )
 
     def project(vector, block):
-        return jnp.dot(cov[block], vector, preferred_element_type=jnp.float32).T
+        return lax.dot_general(
+            vector, cov[block], (((1,), (1,)), ((), ())), preferred_element_type=jnp.float32
+        )
 
     def reduce_users(phase, vector, send, recv):
-        vector = vector.T.astype(jnp.bfloat16)
+        vector = vector.astype(jnp.bfloat16)
 
         def for_sibling(i):
             if phase == 0:
@@ -149,14 +160,14 @@
 
         for_sibling(0)
         for_sibling(1)
-        lax.fori_loop(0, chips - 2, both, 0)
+        loop(0, chips - 2, both, 0)
         send_own(chips - 2)
 
         def add(i, total):
             rs_copy(phase, send, recv, i).wait_recv()
             return total + recv[i].astype(jnp.float32)
 
-        return lax.fori_loop(0, chips - 1, add, for_own(chips - 1))
+        return loop(0, chips - 1, add, for_own(chips - 1))
 
     def ag_copy(phase, s):
         peer = sibling if s is None else chip_after(s) * 2 + core
@@ -190,7 +201,7 @@
             ag_copy(phase, s).start()
             return carry
 
-        lax.fori_loop(1, chips, send, 0)
+        loop(1, chips, send, 0)
 
         def term(block_values, block):
             return jnp.dot(block_values, cov[block], preferred_element_type=jnp.float32)
@@ -210,7 +221,7 @@
         total = term(values, me)
         ag_copy(phase, None).wait_recv()
         total = total + term(share_recv[phase, 0], sibling) + direct(1)
-        total = lax.fori_loop(1, chips - 1, both, total)
+        total = loop(1, chips - 1, both, total)
         if meanwhile is not None:
             meanwhile()
         row_buf[phase, my_row] = total + passed(chips - 1)
@@ -223,8 +234,8 @@
             row_copy(phase, t, lax.rem(my_row + rows - t, rows)).wait_recv()
             return carry
 
-        lax.fori_loop(1, rows, send_row, 0)
-        lax.fori_loop(1, rows, wait_row, 0)
+        loop(1, rows, send_row, 0)
+        loop(1, rows, wait_row, 0)
         total = row_buf[phase, 0]
         for r in range(1, rows):
             total = total + row_buf[phase, r]
@@ -245,14 +256,14 @@
             dot_copy(phase, j).start()
             return carry
 
-        lax.fori_loop(1, n, send, 0)
+        loop(1, n, send, 0)
 
     def take_dots(phase, tiles):
         def add(j, totals):
             dot_copy(phase, j).wait_recv()
             return tuple(total + dot_recv[phase, j, k] for k, total in enumerate(totals))
 
-        totals = lax.fori_loop(1, n, add, tuple(dot_send[phase, k] for k in range(tiles)))
+        totals = loop(1, n, add, tuple(dot_send[phase, k] for k in range(tiles)))
         return [jnp.sum(total, keepdims=True) for total in totals]
 
     def curve_copy(phase, t, slot):
@@ -269,14 +280,14 @@
             curve_copy(phase, t, my_row).start()
             return carry
 
-        lax.fori_loop(1, rows, send, 0)
+        loop(1, rows, send, 0)
 
     def take_curve(phase):
         def wait(t, carry):
             curve_copy(phase, t, lax.rem(my_row + rows - t, rows)).wait_recv()
             return carry
 
-        lax.fori_loop(1, rows, wait, 0)
+        loop(1, rows, wait, 0)
         total = curve_buf[phase, 0]
         for r in range(1, rows):
             total = total + curve_buf[phase, r]
@@ -363,10 +374,10 @@
 
     for phase in range(ITERS):
         ag_copy(phase, None).wait_send()
-    lax.fori_loop(0, chips, drain_pair, 0)
-    lax.fori_loop(1, chips, drain_chip, 0)
-    lax.fori_loop(1, n, drain_col, 0)
-    lax.fori_loop(1, rows, drain_row, 0)
+    loop(0, chips, drain_pair, 0)
+    loop(1, chips, drain_chip, 0)
+    loop(1, n, drain_col, 0)
+    loop(1, rows, drain_row, 0)
 
 
 def body(covariates, labels, weights, sample_index):

time: 64.6 us -> 62.9 us (0.974)
  Pallas kernels: 61 us -> 59.3 us
    pallas_call x1, Pallas kernels: 61 us -> 59.3 us  [body(): pl.pallas_call(functools.partial(kernel, n, rows, users * rows, sub * row...]
where the time goes in v5:
time: 62.9 us; the launch traced here: 62.7 us
  Pallas kernels  59.3 us (94%)
  local copies, waits for them, and re-layouts  2.75 us (4%)
  between operations  0.64 us (1%)
    pallas_call x1, Pallas kernels, body(): pl.pallas_call(functools.partial(kernel, n, rows, users * rows, sub * row...  59.3 us
    unnamed x2, local copies, waits for them, and re-layouts  2.75 us

profile of v5, /device:TPU:0, one launch (start us, length us, event | category | flops | bytes accessed | tf_op | source)
XLA Modules:
  0.0 62.7 jit_solution(1006179364095264976)
XLA Ops:
  0.6 59.3 %newton_step.1 = (f32[16,512]{1,0:T(8,128)}, f32[16,512]{1,0:T(8,128)}) custom-call(bf16[8,1024,512]{2,1,0:T(8,128)(2,1)} %bitcast.3, s32[8,1,1024]{2,1,0:T(1,128)} %bitcast.4, f32[16,512]{1,0:T(8,128)} %weights_hbm.1, s32[1,4096]{1,0:T(1,128)} %bitcast.5), custom_call_target="tpu_custom_call" | custom-call | tf_op jit(solution)/shard_map/newton_step/pallas_call | solution.py:391
  59.9 1.4 %copy.8 = f32[16,512]{1,0:T(8,128)} copy(f32[16,512]{1,0:T(8,128)} %get-tuple-element.4) | data formatting | bytes 65536
  61.3 1.4 %copy.9 = f32[16,512]{1,0:T(8,128)} copy(f32[16,512]{1,0:T(8,128)} %get-tuple-element.5) | data formatting | bytes 65536

commit v6 on v4

--- a/solution.py
+++ b/solution.py
@@ -25,7 +25,7 @@
     n, rows, user_total, sub_total,
     cov_hbm, labels_hbm, weights_hbm, index_hbm, gradient_ref, step_ref,
     cov, labels_ref, weights_ref, index_ref, pair_send, pair_recv, logit_send, logit_recv, resp_send, resp_recv,
-    share_send, share_recv, pass_recv, row_buf, curve_buf, dot_send, dot_recv,
+    chip_sum, got, row_buf, curve_buf, dot_send, dot_recv,
     cov_sem, small_sem, pair_ssem, pair_rsem, rs_ssem, rs_rsem, ag_ssem, ag_rsem, pass_ssem, pass_rsem,
     row_ssem, row_rsem, curve_ssem, curve_rsem, dot_ssem, dot_rsem,
 ):
@@ -47,15 +47,27 @@
     def chip_before(s):
         return lax.rem(chip + chips - s, chips)
 
-    def theirs(i):
-        return chip_after(chips - 1 - i) * 2 + 1 - core
-
     def mine(i):
         return chip_after(chips - 1 - i) * 2 + core
 
-    def cov_copy(side, i):
-        block = theirs(i) if side == 0 else mine(i)
-        return pltpu.make_async_copy(cov_hbm.at[block], cov.at[block], cov_sem.at[side, i])
+    def send_order(u):
+        first, last, odd = (n - 1 - u) // (n - 1), u // (n - 1), lax.rem(u, 2)
+        side = 1 - first - odd * (1 - last)
+        i = odd * (1 - last) * ((u + 1) // 2) + last * (chips - 1) + (1 - odd) * (1 - first) * ((u + first) // 2 - 1 + first)
+        return side, i
+
+    def take_order(u):
+        last, odd, late = u // (n - 1), lax.rem(u, 2), (u + n - 3) // n
+        side = late * (last + (1 - odd)) + (1 - late) * odd
+        s = late * (last * (chips - 1) + odd * (1 - last) * ((u + 1) // 2) + (1 - odd) * (u // 2 - 1)) + (1 - late) * (u // 2)
+        return side, s
+
+    def send_block(side, i):
+        return chip_after(chips - 1 - i) * 2 + side * core + (1 - side) * (1 - core)
+
+    def cov_copy(u):
+        block = send_block(*send_order(u))
+        return pltpu.make_async_copy(cov_hbm.at[block], cov.at[block], cov_sem.at[u])
 
     small_copies = [
         pltpu.make_async_copy(weights_hbm, weights_ref, small_sem.at[0]),
@@ -65,12 +77,11 @@
     for copy in small_copies:
         copy.start()
 
-    def start_cov(i, carry):
-        cov_copy(0, i).start()
-        cov_copy(1, i).start()
-        return carry
-
-    lax.fori_loop(0, chips, start_cov, 0)
+    def start_cov(u, carry):
+        cov_copy(u).start()
+        return carry
+
+    lax.fori_loop(0, n, start_cov, 0)
 
     barrier = pltpu.get_barrier_semaphore()
 
@@ -120,56 +131,54 @@
         )
 
     def project(vector, block):
-        return jnp.dot(cov[block], vector, preferred_element_type=jnp.float32).T
+        return lax.dot_general(
+            vector, cov[block], (((1,), (1,)), ((), ())), preferred_element_type=jnp.float32
+        )
 
     def reduce_users(phase, vector, send, recv):
-        vector = vector.T.astype(jnp.bfloat16)
-
-        def for_sibling(i):
+        vector = vector.astype(jnp.bfloat16)
+
+        def one(u, carry):
+            side, i = send_order(u)
             if phase == 0:
-                cov_copy(0, i).wait()
-            pair_send[phase, i] = project(vector, theirs(i))
-            pair_copy(phase, i).start()
-
-        def for_own(i):
-            if phase == 0:
-                cov_copy(1, i).wait()
-            part = project(vector, mine(i))
-            pair_copy(phase, i).wait_recv()
-            return part + pair_recv[phase, i]
-
-        def send_own(i):
-            send[i] = for_own(i).astype(send.dtype)
-            rs_copy(phase, send, recv, i).start()
-
-        def both(i, carry):
-            send_own(i)
-            for_sibling(i + 2)
-            return carry
-
-        for_sibling(0)
-        for_sibling(1)
-        lax.fori_loop(0, chips - 2, both, 0)
-        send_own(chips - 2)
+                cov_copy(u).wait()
+            part = project(vector, send_block(side, i))
+
+            @pl.when(side == 0)
+            def _():
+                pair_send[phase, i] = part
+                pair_copy(phase, i).start()
+
+            @pl.when(side == 1)
+            def _():
+                pair_copy(phase, i).wait_recv()
+                chip_sum[...] = part + pair_recv[phase, i]
+
+                @pl.when(i < chips - 1)
+                def _():
+                    send[i] = chip_sum[...].astype(send.dtype)
+                    rs_copy(phase, send, recv, i).start()
+
+            return carry
+
+        lax.fori_loop(0, n, one, 0)
 
         def add(i, total):
             rs_copy(phase, send, recv, i).wait_recv()
             return total + recv[i].astype(jnp.float32)
 
-        return lax.fori_loop(0, chips - 1, add, for_own(chips - 1))
+        return lax.fori_loop(0, chips - 1, add, chip_sum[...])
 
     def ag_copy(phase, s):
-        peer = sibling if s is None else chip_after(s) * 2 + core
-        slot = 0 if s is None else s
-        return pltpu.make_async_remote_copy(
-            src_ref=share_send.at[phase], dst_ref=share_recv.at[phase, slot],
-            send_sem=ag_ssem.at[phase, slot], recv_sem=ag_rsem.at[phase, slot],
-            device_id={"col": peer}, device_id_type=MESH,
+        return pltpu.make_async_remote_copy(
+            src_ref=got.at[phase, 0, 0], dst_ref=got.at[phase, 0, s],
+            send_sem=ag_ssem.at[phase, s], recv_sem=ag_rsem.at[phase, s],
+            device_id={"col": chip_after(s) * 2 + core}, device_id_type=MESH,
         )
 
     def forward(phase, s):
         return pltpu.make_async_remote_copy(
-            src_ref=share_recv.at[phase, s], dst_ref=pass_recv.at[phase, s],
+            src_ref=got.at[phase, 0, s], dst_ref=got.at[phase, 1, s],
             send_sem=pass_ssem.at[phase, s], recv_sem=pass_rsem.at[phase, s],
             device_id={"col": sibling}, device_id_type=MESH,
         )
@@ -182,9 +191,8 @@
         )
 
     def back_project(phase, values, meanwhile=None):
-        share_send[phase] = values
-
-        ag_copy(phase, None).start()
+        got[phase, 0, 0] = values
+        forward(phase, 0).start()
 
         def send(s, carry):
             ag_copy(phase, s).start()
@@ -192,28 +200,25 @@
 
         lax.fori_loop(1, chips, send, 0)
 
-        def term(block_values, block):
-            return jnp.dot(block_values, cov[block], preferred_element_type=jnp.float32)
-
-        def direct(s):
-            ag_copy(phase, s).wait_recv()
-            forward(phase, s).start()
-            return term(share_recv[phase, s], chip_before(s) * 2 + core)
-
-        def passed(s):
-            forward(phase, s).wait_recv()
-            return term(pass_recv[phase, s], chip_before(s) * 2 + 1 - core)
-
-        def both(s, total):
-            return total + direct(s + 1) + passed(s)
-
-        total = term(values, me)
-        ag_copy(phase, None).wait_recv()
-        total = total + term(share_recv[phase, 0], sibling) + direct(1)
-        total = lax.fori_loop(1, chips - 1, both, total)
+        def add(u, total):
+            side, s = take_order(u)
+
+            @pl.when(side == 1)
+            def _():
+                forward(phase, s).wait_recv()
+
+            @pl.when(jnp.logical_and(side == 0, s > 0))
+            def _():
+                ag_copy(phase, s).wait_recv()
+                forward(phase, s).start()
+
+            block = chip_before(s) * 2 + (1 - side) * core + side * (1 - core)
+            return total + jnp.dot(got[phase, side, s], cov[block], preferred_element_type=jnp.float32)
+
+        total = lax.fori_loop(0, n - 1, add, jnp.zeros(weights_ref.shape, jnp.float32))
         if meanwhile is not None:
             meanwhile()
-        row_buf[phase, my_row] = total + passed(chips - 1)
+        row_buf[phase, my_row] = add(n - 1, total)
 
         def send_row(t, carry):
             row_copy(phase, t, my_row).start()
@@ -362,7 +367,7 @@
         return carry
 
     for phase in range(ITERS):
-        ag_copy(phase, None).wait_send()
+        forward(phase, 0).wait_send()
     lax.fori_loop(0, chips, drain_pair, 0)
     lax.fori_loop(1, chips, drain_chip, 0)
     lax.fori_loop(1, n, drain_col, 0)
@@ -393,14 +398,13 @@
             pltpu.VMEM((chips, classes, own), jnp.float32),
             pltpu.VMEM((ITERS, chips, classes, own), jnp.bfloat16),
             pltpu.VMEM((ITERS, chips, classes, own), jnp.bfloat16),
-            pltpu.VMEM((ITERS, classes, own), jnp.bfloat16),
-            pltpu.VMEM((ITERS, chips, classes, own), jnp.bfloat16),
-            pltpu.VMEM((ITERS, chips, classes, own), jnp.bfloat16),
+            pltpu.VMEM((classes, own), jnp.float32),
+            pltpu.VMEM((ITERS, 2, chips, classes, own), jnp.bfloat16),
             pltpu.VMEM((ITERS, rows, classes, width), jnp.float32),
             pltpu.VMEM((ITERS, rows, 8, LANES), jnp.float32),
             pltpu.VMEM((dots, 2, 8, LANES), jnp.float32),
             pltpu.VMEM((dots, n, 2, 8, LANES), jnp.float32),
-            dma((2, chips)), dma((3,)),
+            dma((n,)), dma((3,)),
             dma((ITERS + 1, chips)), dma((ITERS + 1, chips)),
             dma((ITERS + 1, chips)), dma((ITERS + 1, chips)),
             dma((ITERS, chips)), dma((ITERS, chips)),

time: 64.6 us -> 61.8 us (0.957)
  Pallas kernels: 61 us -> 58.1 us
    pallas_call x1, Pallas kernels: 61 us -> 58.1 us  [body(): pl.pallas_call(functools.partial(kernel, n, rows, users * rows, sub * row...]
where the time goes in v6:
time: 61.8 us; the launch traced here: 61.5 us
  Pallas kernels  58.1 us (94%)
  local copies, waits for them, and re-layouts  2.75 us (4%)
  between operations  0.64 us (1%)
    pallas_call x1, Pallas kernels, body(): pl.pallas_call(functools.partial(kernel, n, rows, users * rows, sub * row...  58.1 us
    unnamed x2, local copies, waits for them, and re-layouts  2.75 us

profile of v6, /device:TPU:0, one launch (start us, length us, event | category | flops | bytes accessed | tf_op | source)
XLA Modules:
  0.0 61.5 jit_solution(1495345461538754057)
XLA Ops:
  0.6 58.1 %newton_step.1 = (f32[16,512]{1,0:T(8,128)}, f32[16,512]{1,0:T(8,128)}) custom-call(bf16[8,1024,512]{2,1,0:T(8,128)(2,1)} %bitcast.3, s32[8,1,1024]{2,1,0:T(1,128)} %bitcast.4, f32[16,512]{1,0:T(8,128)} %weights_hbm.1, s32[1,4096]{1,0:T(1,128)} %bitcast.5), custom_call_target="tpu_custom_call" | custom-call | tf_op jit(solution)/shard_map/newton_step/pallas_call | solution.py:385
  58.8 1.4 %copy.8 = f32[16,512]{1,0:T(8,128)} copy(f32[16,512]{1,0:T(8,128)} %get-tuple-element.4) | data formatting | bytes 65536
  60.2 1.4 %copy.9 = f32[16,512]{1,0:T(8,128)} copy(f32[16,512]{1,0:T(8,128)} %get-tuple-element.5) | data formatting | bytes 65536

commit v7 on v6

--- a/solution.py
+++ b/solution.py
@@ -10,6 +10,7 @@
 ITERS = 2
 RIDGE_WEIGHT = 0.004
 LANES = 128
+PARTS = 2
 MESH = pl.DeviceIdType.MESH
 
 
@@ -33,6 +34,7 @@
     my_row = lax.axis_index("row")
     chips = n // 2
     own = cov.shape[1]
+    half = own // PARTS
     classes = weights_ref.shape[0]
 
     chip, core = me // 2, lax.rem(me, 2)
@@ -65,9 +67,14 @@
     def send_block(side, i):
         return chip_after(chips - 1 - i) * 2 + side * core + (1 - side) * (1 - core)
 
-    def cov_copy(u):
+    def users(h):
+        return pl.ds(h * half, half)
+
+    def cov_copy(u, h):
         block = send_block(*send_order(u))
-        return pltpu.make_async_copy(cov_hbm.at[block], cov.at[block], cov_sem.at[u])
+        return pltpu.make_async_copy(
+            cov_hbm.at[block, users(h)], cov.at[block, users(h)], cov_sem.at[h, u]
+        )
 
     small_copies = [
         pltpu.make_async_copy(weights_hbm, weights_ref, small_sem.at[0]),
@@ -77,11 +84,13 @@
     for copy in small_copies:
         copy.start()
 
-    def start_cov(u, carry):
-        cov_copy(u).start()
-        return carry
-
-    lax.fori_loop(0, n, start_cov, 0)
+    for h in range(PARTS):
+
+        def start_cov(u, carry):
+            cov_copy(u, h).start()
+            return carry
+
+        lax.fori_loop(0, n, start_cov, 0)
 
     barrier = pltpu.get_barrier_semaphore()
 
@@ -116,72 +125,89 @@
 
     pl.semaphore_wait(barrier, n - 1 + rows - 1)
 
-    def pair_copy(phase, i):
-        return pltpu.make_async_remote_copy(
-            src_ref=pair_send.at[phase, i], dst_ref=pair_recv.at[phase, i],
-            send_sem=pair_ssem.at[phase, i], recv_sem=pair_rsem.at[phase, i],
+    def pair_copy(phase, h, i):
+        return pltpu.make_async_remote_copy(
+            src_ref=pair_send.at[phase, h, i], dst_ref=pair_recv.at[phase, h, i],
+            send_sem=pair_ssem.at[phase, h, i], recv_sem=pair_rsem.at[phase, h, i],
             device_id={"col": sibling}, device_id_type=MESH,
         )
 
-    def rs_copy(phase, send, recv, i):
-        return pltpu.make_async_remote_copy(
-            src_ref=send.at[i], dst_ref=recv.at[i],
-            send_sem=rs_ssem.at[phase, i], recv_sem=rs_rsem.at[phase, i],
+    def rs_refs(phase):
+        return (logit_send, logit_recv) if phase == 0 else (resp_send.at[phase - 1], resp_recv.at[phase - 1])
+
+    def rs_copy(phase, h, i):
+        send, recv = rs_refs(phase)
+        return pltpu.make_async_remote_copy(
+            src_ref=send.at[h, i], dst_ref=recv.at[h, i],
+            send_sem=rs_ssem.at[phase, h, i], recv_sem=rs_rsem.at[phase, h, i],
             device_id={"col": mine(i)}, device_id_type=MESH,
         )
 
-    def project(vector, block):
-        return lax.dot_general(
-            vector, cov[block], (((1,), (1,)), ((), ())), preferred_element_type=jnp.float32
-        )
-
-    def reduce_users(phase, vector, send, recv):
+    def start_reduce(phase, vector):
         vector = vector.astype(jnp.bfloat16)
-
-        def one(u, carry):
-            side, i = send_order(u)
-            if phase == 0:
-                cov_copy(u).wait()
-            part = project(vector, send_block(side, i))
-
-            @pl.when(side == 0)
-            def _():
-                pair_send[phase, i] = part
-                pair_copy(phase, i).start()
-
-            @pl.when(side == 1)
-            def _():
-                pair_copy(phase, i).wait_recv()
-                chip_sum[...] = part + pair_recv[phase, i]
-
-                @pl.when(i < chips - 1)
+        send = rs_refs(phase)[0]
+        for h in range(PARTS):
+
+            def one(u, carry):
+                side, i = send_order(u)
+                if phase == 0:
+                    cov_copy(u, h).wait()
+                part = lax.dot_general(
+                    vector, cov[send_block(side, i), users(h)], (((1,), (1,)), ((), ())),
+                    preferred_element_type=jnp.float32,
+                )
+
+                @pl.when(side == 0)
                 def _():
-                    send[i] = chip_sum[...].astype(send.dtype)
-                    rs_copy(phase, send, recv, i).start()
-
-            return carry
-
-        lax.fori_loop(0, n, one, 0)
+                    pair_send[phase, h, i] = part
+                    pair_copy(phase, h, i).start()
+
+                @pl.when(side == 1)
+                def _():
+                    pair_copy(phase, h, i).wait_recv()
+                    chip_sum[h] = part + pair_recv[phase, h, i]
+
+                    @pl.when(i < chips - 1)
+                    def _():
+                        send[h, i] = chip_sum[h].astype(send.dtype)
+                        rs_copy(phase, h, i).start()
+
+                return carry
+
+            lax.fori_loop(0, n, one, 0)
+
+    def end_reduce(phase, h):
+        recv = rs_refs(phase)[1]
 
         def add(i, total):
-            rs_copy(phase, send, recv, i).wait_recv()
-            return total + recv[i].astype(jnp.float32)
-
-        return lax.fori_loop(0, chips - 1, add, chip_sum[...])
-
-    def ag_copy(phase, s):
-        return pltpu.make_async_remote_copy(
-            src_ref=got.at[phase, 0, 0], dst_ref=got.at[phase, 0, s],
-            send_sem=ag_ssem.at[phase, s], recv_sem=ag_rsem.at[phase, s],
+            rs_copy(phase, h, i).wait_recv()
+            return total + recv[h, i].astype(jnp.float32)
+
+        return lax.fori_loop(0, chips - 1, add, chip_sum[h])
+
+    def ag_copy(phase, h, s):
+        return pltpu.make_async_remote_copy(
+            src_ref=got.at[phase, h, 0, 0], dst_ref=got.at[phase, h, 0, s],
+            send_sem=ag_ssem.at[phase, h, s], recv_sem=ag_rsem.at[phase, h, s],
             device_id={"col": chip_after(s) * 2 + core}, device_id_type=MESH,
         )
 
-    def forward(phase, s):
-        return pltpu.make_async_remote_copy(
-            src_ref=got.at[phase, 0, s], dst_ref=got.at[phase, 1, s],
-            send_sem=pass_ssem.at[phase, s], recv_sem=pass_rsem.at[phase, s],
+    def forward(phase, h, s):
+        return pltpu.make_async_remote_copy(
+            src_ref=got.at[phase, h, 0, s], dst_ref=got.at[phase, h, 1, s],
+            send_sem=pass_ssem.at[phase, h, s], recv_sem=pass_rsem.at[phase, h, s],
             device_id={"col": sibling}, device_id_type=MESH,
         )
+
+    def give(phase, h, values):
+        got[phase, h, 0, 0] = values
+        forward(phase, h, 0).start()
+
+        def send(s, carry):
+            ag_copy(phase, h, s).start()
+            return carry
+
+        lax.fori_loop(1, chips, send, 0)
 
     def row_copy(phase, t, slot):
         return pltpu.make_async_remote_copy(
@@ -190,35 +216,31 @@
             device_id={"row": lax.rem(my_row + t, rows)}, device_id_type=MESH,
         )
 
-    def back_project(phase, values, meanwhile=None):
-        got[phase, 0, 0] = values
-        forward(phase, 0).start()
-
-        def send(s, carry):
-            ag_copy(phase, s).start()
-            return carry
-
-        lax.fori_loop(1, chips, send, 0)
-
-        def add(u, total):
-            side, s = take_order(u)
-
-            @pl.when(side == 1)
-            def _():
-                forward(phase, s).wait_recv()
-
-            @pl.when(jnp.logical_and(side == 0, s > 0))
-            def _():
-                ag_copy(phase, s).wait_recv()
-                forward(phase, s).start()
-
-            block = chip_before(s) * 2 + (1 - side) * core + side * (1 - core)
-            return total + jnp.dot(got[phase, side, s], cov[block], preferred_element_type=jnp.float32)
-
-        total = lax.fori_loop(0, n - 1, add, jnp.zeros(weights_ref.shape, jnp.float32))
-        if meanwhile is not None:
-            meanwhile()
-        row_buf[phase, my_row] = add(n - 1, total)
+    def back_project(phase, meanwhile=None):
+        total = jnp.zeros(weights_ref.shape, jnp.float32)
+        for h in range(PARTS):
+
+            def add(u, total):
+                side, s = take_order(u)
+
+                @pl.when(side == 1)
+                def _():
+                    forward(phase, h, s).wait_recv()
+
+                @pl.when(jnp.logical_and(side == 0, s > 0))
+                def _():
+                    ag_copy(phase, h, s).wait_recv()
+                    forward(phase, h, s).start()
+
+                block = chip_before(s) * 2 + (1 - side) * core + side * (1 - core)
+                return total + jnp.dot(
+                    got[phase, h, side, s], cov[block, users(h)], preferred_element_type=jnp.float32
+                )
+
+            total = lax.fori_loop(0, n, add, total)
+            if h == 0 and meanwhile is not None:
+                meanwhile()
+        row_buf[phase, my_row] = total
 
         def send_row(t, carry):
             row_copy(phase, t, my_row).start()
@@ -288,38 +310,45 @@
         return total
 
     weights = weights_ref[...]
-    logits = reduce_users(0, weights, logit_send, logit_recv)
-    exponent = jnp.exp(logits)
-    shares = exponent / jnp.sum(exponent, axis=0, keepdims=True)
-    label = labels_ref[...]
-    indicator = (label == lax.broadcasted_iota(jnp.int32, (classes, own), 0)).astype(jnp.float32)
-    misfit = (shares - indicator).astype(jnp.bfloat16)
-    gradient = back_project(0, misfit) / user_total + RIDGE_WEIGHT * weights
+    start_reduce(0, weights)
+    shares, counted = [], []
+    for h in range(PARTS):
+        exponent = jnp.exp(end_reduce(0, h))
+        shares.append(exponent / jnp.sum(exponent, axis=0, keepdims=True))
+        label = labels_ref[:, h * half:(h + 1) * half]
+        indicator = (label == lax.broadcasted_iota(jnp.int32, (classes, half), 0)).astype(jnp.float32)
+        give(0, h, (shares[h] - indicator).astype(jnp.bfloat16))
+        counted.append(count[:, h * half:(h + 1) * half] * shares[h])
+    gradient = back_project(0) / user_total + RIDGE_WEIGHT * weights
     gradient_ref[...] = gradient
-    counted = count * shares
 
     residual = -gradient
     direction = residual
     newton_step = jnp.zeros_like(residual)
-    norm_now = step_size = image = residual_response = direction_response = None
+    norm_now = step_size = image = None
+    residual_response, direction_response = [None] * PARTS, [None] * PARTS
     for iteration in range(ITERS):
         last = iteration + 1 == ITERS
-        vector = direction if iteration == 0 else image
-        response = reduce_users(
-            iteration + 1, vector, resp_send.at[iteration], resp_recv.at[iteration]
-        )
-        if iteration == 0:
-            residual_response = direction_response = response
-        else:
+        start_reduce(iteration + 1, direction if iteration == 0 else image)
+        if iteration > 0:
             (norm_new,) = take_dots(2 * iteration - 1, 1)
             ratio = norm_new / norm_now
             direction = residual + ratio * direction
             norm_now = norm_new
-            residual_response = residual_response - step_size * response
-            direction_response = residual_response + ratio * direction_response
-        centred = direction_response - jnp.sum(shares * direction_response, axis=0, keepdims=True)
-        weighted = (counted * centred).astype(jnp.bfloat16)
-        send_curve(iteration, fold(weighted.astype(jnp.float32) * direction_response))
+        curve_tile = jnp.zeros((8, LANES), jnp.float32)
+        for h in range(PARTS):
+            response = end_reduce(iteration + 1, h)
+            if iteration == 0:
+                residual_response[h] = direction_response[h] = response
+            else:
+                residual_response[h] = residual_response[h] - step_size * response
+                direction_response[h] = residual_response[h] + ratio * direction_response[h]
+            centred = direction_response[h] - jnp.sum(shares[h] * direction_response[h], axis=0, keepdims=True)
+            weighted = (counted[h] * centred).astype(jnp.bfloat16)
+            if not last:
+                give(iteration + 1, h, weighted)
+            curve_tile = curve_tile + fold(weighted.astype(jnp.float32) * direction_response[h])
+        send_curve(iteration, curve_tile)
         square = fold(direction * direction)
 
         def pass_curve():
@@ -329,7 +358,7 @@
         if last:
             pass_curve()
         else:
-            image = back_project(iteration + 1, weighted, pass_curve) / sub_total + RIDGE_WEIGHT * direction
+            image = back_project(iteration + 1, pass_curve) / sub_total + RIDGE_WEIGHT * direction
         if iteration == 0:
             curve, norm_now = take_dots(0, 2)
         else:
@@ -341,18 +370,20 @@
             send_dots(2 * iteration + 1, fold(residual * residual))
     step_ref[...] = newton_step
 
-    def drain_pair(i, carry):
-        for phase in range(ITERS + 1):
-            pair_copy(phase, i).wait_send()
-        return carry
-
     def drain_chip(s, carry):
-        rs_copy(0, logit_send, logit_recv, s - 1).wait_send()
-        for phase in range(ITERS):
-            rs_copy(phase + 1, resp_send.at[phase], resp_recv.at[phase], s - 1).wait_send()
-        for phase in range(ITERS):
-            ag_copy(phase, s).wait_send()
-            forward(phase, s).wait_send()
+        for h in range(PARTS):
+            for phase in range(ITERS + 1):
+                pair_copy(phase, h, s).wait_send()
+            for phase in range(ITERS):
+                forward(phase, h, s).wait_send()
+
+            @pl.when(s > 0)
+            def _():
+                for phase in range(ITERS + 1):
+                    rs_copy(phase, h, s - 1).wait_send()
+                for phase in range(ITERS):
+                    ag_copy(phase, h, s).wait_send()
+
         return carry
 
     def drain_col(j, carry):
@@ -366,10 +397,7 @@
             curve_copy(phase, t, my_row).wait_send()
         return carry
 
-    for phase in range(ITERS):
-        forward(phase, 0).wait_send()
-    lax.fori_loop(0, chips, drain_pair, 0)
-    lax.fori_loop(1, chips, drain_chip, 0)
+    lax.fori_loop(0, chips, drain_chip, 0)
     lax.fori_loop(1, n, drain_col, 0)
     lax.fori_loop(1, rows, drain_row, 0)
 
@@ -378,6 +406,7 @@
     users, width = covariates.shape
     n, rows = lax.axis_size("col"), lax.axis_size("row")
     own, chips = users // n, n // 2
+    half = own // PARTS
     classes = weights.shape[0]
     sub = sample_index.shape[0]
     dots = 2 * ITERS - 1
@@ -392,23 +421,23 @@
             pltpu.VMEM((1, own), jnp.int32),
             pltpu.VMEM((classes, width), jnp.float32),
             pltpu.VMEM((1, sub), jnp.int32),
-            pltpu.VMEM((ITERS + 1, chips, classes, own), jnp.float32),
-            pltpu.VMEM((ITERS + 1, chips, classes, own), jnp.float32),
-            pltpu.VMEM((chips, classes, own), jnp.float32),
-            pltpu.VMEM((chips, classes, own), jnp.float32),
-            pltpu.VMEM((ITERS, chips, classes, own), jnp.bfloat16),
-            pltpu.VMEM((ITERS, chips, classes, own), jnp.bfloat16),
-            pltpu.VMEM((classes, own), jnp.float32),
-            pltpu.VMEM((ITERS, 2, chips, classes, own), jnp.bfloat16),
+            pltpu.VMEM((ITERS + 1, PARTS, chips, classes, half), jnp.float32),
+            pltpu.VMEM((ITERS + 1, PARTS, chips, classes, half), jnp.float32),
+            pltpu.VMEM((PARTS, chips, classes, half), jnp.float32),
+            pltpu.VMEM((PARTS, chips, classes, half), jnp.float32),
+            pltpu.VMEM((ITERS, PARTS, chips, classes, half), jnp.bfloat16),
+            pltpu.VMEM((ITERS, PARTS, chips, classes, half), jnp.bfloat16),
+            pltpu.VMEM((PARTS, classes, half), jnp.float32),
+            pltpu.VMEM((ITERS, PARTS, 2, chips, classes, half), jnp.bfloat16),
             pltpu.VMEM((ITERS, rows, classes, width), jnp.float32),
             pltpu.VMEM((ITERS, rows, 8, LANES), jnp.float32),
             pltpu.VMEM((dots, 2, 8, LANES), jnp.float32),
             pltpu.VMEM((dots, n, 2, 8, LANES), jnp.float32),
-            dma((n,)), dma((3,)),
-            dma((ITERS + 1, chips)), dma((ITERS + 1, chips)),
-            dma((ITERS + 1, chips)), dma((ITERS + 1, chips)),
-            dma((ITERS, chips)), dma((ITERS, chips)),
-            dma((ITERS, chips)), dma((ITERS, chips)),
+            dma((PARTS, n)), dma((3,)),
+            dma((ITERS + 1, PARTS, chips)), dma((ITERS + 1, PARTS, chips)),
+            dma((ITERS + 1, PARTS, chips)), dma((ITERS + 1, PARTS, chips)),
+            dma((ITERS, PARTS, chips)), dma((ITERS, PARTS, chips)),
+            dma((ITERS, PARTS, chips)), dma((ITERS, PARTS, chips)),
             dma((ITERS, rows)), dma((ITERS, rows)),
             dma((ITERS, rows)), dma((ITERS, rows)),
             dma((dots, n)), dma((dots, n)),

time: 61.8 us -> 65.5 us (1.060)
  Pallas kernels: 58.1 us -> 61.9 us
    pallas_call x1, Pallas kernels: 58.1 us -> 61.9 us  [body(): pl.pallas_call(functools.partial(kernel, n, rows, users * rows, sub * row...]
where the time goes in v7:
time: 65.5 us; the launch traced here: 65.2 us
  Pallas kernels  61.9 us (95%)
  local copies, waits for them, and re-layouts  2.75 us (4%)
    pallas_call x1, Pallas kernels, body(): pl.pallas_call(functools.partial(kernel, n, rows, users * rows, sub * row...  61.9 us
    unnamed x2, local copies, waits for them, and re-layouts  2.75 us

profile of v7, /device:TPU:0, one launch (start us, length us, event | category | flops | bytes accessed | tf_op | source)
XLA Modules:
  0.0 65.2 jit_solution(11970153021995158744)
XLA Ops:
  0.6 61.9 %newton_step.1 = (f32[16,512]{1,0:T(8,128)}, f32[16,512]{1,0:T(8,128)}) custom-call(bf16[8,1024,512]{2,1,0:T(8,128)(2,1)} %bitcast.3, s32[8,1,1024]{2,1,0:T(1,128)} %bitcast.4, f32[16,512]{1,0:T(8,128)} %weights_hbm.1, s32[1,4096]{1,0:T(1,128)} %bitcast.5), custom_call_target="tpu_custom_call" | custom-call | tf_op jit(solution)/shard_map/newton_step/pallas_call | solution.py:414
  62.5 1.4 %copy.8 = f32[16,512]{1,0:T(8,128)} copy(f32[16,512]{1,0:T(8,128)} %get-tuple-element.4) | data formatting | bytes 65536
  63.9 1.4 %copy.9 = f32[16,512]{1,0:T(8,128)} copy(f32[16,512]{1,0:T(8,128)} %get-tuple-element.5) | data formatting | bytes 65536

commit v8 on v6

--- a/solution.py
+++ b/solution.py
@@ -32,11 +32,12 @@
     me = lax.axis_index("col")
     my_row = lax.axis_index("row")
     chips = n // 2
-    own = cov.shape[1]
+    pairs, own = cov.shape[1], cov.shape[2] // 2
     classes = weights_ref.shape[0]
 
     chip, core = me // 2, lax.rem(me, 2)
     sibling = chip * 2 + 1 - core
+    own_block = core * chips + chip
 
     def target(j):
         return lax.rem(me + j, n)
@@ -47,32 +48,22 @@
     def chip_before(s):
         return lax.rem(chip + chips - s, chips)
 
-    def mine(i):
-        return chip_after(chips - 1 - i) * 2 + core
-
     def send_order(u):
-        first, last, odd = (n - 1 - u) // (n - 1), u // (n - 1), lax.rem(u, 2)
-        side = 1 - first - odd * (1 - last)
-        i = odd * (1 - last) * ((u + 1) // 2) + last * (chips - 1) + (1 - odd) * (1 - first) * ((u + first) // 2 - 1 + first)
-        return side, i
-
-    def take_order(u):
-        last, odd, late = u // (n - 1), lax.rem(u, 2), (u + n - 3) // n
-        side = late * (last + (1 - odd)) + (1 - late) * odd
-        s = late * (last * (chips - 1) + odd * (1 - last) * ((u + 1) // 2) + (1 - odd) * (u // 2 - 1)) + (1 - late) * (u // 2)
-        return side, s
-
-    def send_block(side, i):
-        return chip_after(chips - 1 - i) * 2 + side * core + (1 - side) * (1 - core)
+        side, i = u // pairs, lax.rem(u, pairs)
+        return side, i, lax.rem(chip // 2 + i + 1, pairs)
+
+    def half_of(side):
+        return side * core + (1 - side) * (1 - core)
 
     def cov_copy(u):
-        block = send_block(*send_order(u))
-        return pltpu.make_async_copy(cov_hbm.at[block], cov.at[block], cov_sem.at[u])
+        side, i, pair = send_order(u)
+        half = half_of(side)
+        return pltpu.make_async_copy(cov_hbm.at[half, pair], cov.at[half, pair], cov_sem.at[u])
 
     small_copies = [
         pltpu.make_async_copy(weights_hbm, weights_ref, small_sem.at[0]),
         pltpu.make_async_copy(index_hbm, index_ref, small_sem.at[1]),
-        pltpu.make_async_copy(labels_hbm.at[me], labels_ref, small_sem.at[2]),
+        pltpu.make_async_copy(labels_hbm.at[own_block], labels_ref, small_sem.at[2]),
     ]
     for copy in small_copies:
         copy.start()
@@ -81,7 +72,7 @@
         cov_copy(u).start()
         return carry
 
-    lax.fori_loop(0, n, start_cov, 0)
+    lax.fori_loop(0, 2 * pairs, start_cov, 0)
 
     barrier = pltpu.get_barrier_semaphore()
 
@@ -103,7 +94,7 @@
 
     groups = own // LANES
     padded = max(16, groups)
-    within = index_ref[...] - my_row * (n * own) - me * own
+    within = index_ref[...] - my_row * (n * own) - own_block * own
     lane = jnp.bitwise_and(within, LANES - 1)
     group = jnp.right_shift(within - lane, 7)
     group_hot = (lax.broadcasted_iota(jnp.int32, (padded, within.shape[1]), 0) == group)
@@ -123,26 +114,23 @@
             device_id={"col": sibling}, device_id_type=MESH,
         )
 
-    def rs_copy(phase, send, recv, i):
-        return pltpu.make_async_remote_copy(
-            src_ref=send.at[i], dst_ref=recv.at[i],
-            send_sem=rs_ssem.at[phase, i], recv_sem=rs_rsem.at[phase, i],
-            device_id={"col": mine(i)}, device_id_type=MESH,
-        )
-
-    def project(vector, block):
-        return lax.dot_general(
-            vector, cov[block], (((1,), (1,)), ((), ())), preferred_element_type=jnp.float32
+    def rs_copy(phase, send, recv, to, slot):
+        return pltpu.make_async_remote_copy(
+            src_ref=send.at[to], dst_ref=recv.at[slot],
+            send_sem=rs_ssem.at[phase, to], recv_sem=rs_rsem.at[phase, slot],
+            device_id={"col": to * 2 + core}, device_id_type=MESH,
         )
 
     def reduce_users(phase, vector, send, recv):
         vector = vector.astype(jnp.bfloat16)
 
         def one(u, carry):
-            side, i = send_order(u)
+            side, i, pair = send_order(u)
             if phase == 0:
                 cov_copy(u).wait()
-            part = project(vector, send_block(side, i))
+            part = lax.dot_general(
+                vector, cov[half_of(side), pair], (((1,), (1,)), ((), ())), preferred_element_type=jnp.float32
+            )
 
             @pl.when(side == 0)
             def _():
@@ -152,34 +140,42 @@
             @pl.when(side == 1)
             def _():
                 pair_copy(phase, i).wait_recv()
-                chip_sum[...] = part + pair_recv[phase, i]
-
-                @pl.when(i < chips - 1)
-                def _():
-                    send[i] = chip_sum[...].astype(send.dtype)
-                    rs_copy(phase, send, recv, i).start()
-
-            return carry
-
-        lax.fori_loop(0, n, one, 0)
-
-        def add(i, total):
-            rs_copy(phase, send, recv, i).wait_recv()
-            return total + recv[i].astype(jnp.float32)
-
-        return lax.fori_loop(0, chips - 1, add, chip_sum[...])
-
-    def ag_copy(phase, s):
-        return pltpu.make_async_remote_copy(
-            src_ref=got.at[phase, 0, 0], dst_ref=got.at[phase, 0, s],
-            send_sem=ag_ssem.at[phase, s], recv_sem=ag_rsem.at[phase, s],
-            device_id={"col": chip_after(s) * 2 + core}, device_id_type=MESH,
-        )
-
-    def forward(phase, s):
-        return pltpu.make_async_remote_copy(
-            src_ref=got.at[phase, 0, s], dst_ref=got.at[phase, 1, s],
-            send_sem=pass_ssem.at[phase, s], recv_sem=pass_rsem.at[phase, s],
+                both = part + pair_recv[phase, i]
+                for h in range(2):
+                    to = pair * 2 + h
+                    value = both[:, h * own:(h + 1) * own]
+
+                    @pl.when(to != chip)
+                    def _():
+                        send[to] = value.astype(send.dtype)
+                        rs_copy(phase, send, recv, to, chip).start()
+
+                    @pl.when(to == chip)
+                    def _():
+                        chip_sum[...] = value
+
+            return carry
+
+        lax.fori_loop(0, 2 * pairs, one, 0)
+
+        def add(s, total):
+            origin = chip_before(s)
+            rs_copy(phase, send, recv, origin, origin).wait_recv()
+            return total + recv[origin].astype(jnp.float32)
+
+        return lax.fori_loop(1, chips, add, chip_sum[...])
+
+    def ag_copy(phase, to, slot):
+        return pltpu.make_async_remote_copy(
+            src_ref=got.at[phase, 0, chip], dst_ref=got.at[phase, 0, slot],
+            send_sem=ag_ssem.at[phase, to], recv_sem=ag_rsem.at[phase, slot],
+            device_id={"col": to * 2 + core}, device_id_type=MESH,
+        )
+
+    def forward(phase, origin):
+        return pltpu.make_async_remote_copy(
+            src_ref=got.at[phase, 0, origin], dst_ref=got.at[phase, 1, origin],
+            send_sem=pass_ssem.at[phase, origin], recv_sem=pass_rsem.at[phase, origin],
             device_id={"col": sibling}, device_id_type=MESH,
         )
 
@@ -191,34 +187,43 @@
         )
 
     def back_project(phase, values, meanwhile=None):
-        got[phase, 0, 0] = values
-        forward(phase, 0).start()
+        got[phase, 0, chip] = values
+        forward(phase, chip).start()
 
         def send(s, carry):
-            ag_copy(phase, s).start()
+            ag_copy(phase, chip_after(s), chip).start()
             return carry
 
         lax.fori_loop(1, chips, send, 0)
 
-        def add(u, total):
-            side, s = take_order(u)
-
-            @pl.when(side == 1)
-            def _():
-                forward(phase, s).wait_recv()
-
-            @pl.when(jnp.logical_and(side == 0, s > 0))
-            def _():
-                ag_copy(phase, s).wait_recv()
-                forward(phase, s).start()
-
-            block = chip_before(s) * 2 + (1 - side) * core + side * (1 - core)
-            return total + jnp.dot(got[phase, side, s], cov[block], preferred_element_type=jnp.float32)
-
-        total = lax.fori_loop(0, n - 1, add, jnp.zeros(weights_ref.shape, jnp.float32))
+        def term(side, pair):
+            both = jnp.concatenate([got[phase, side, pair * 2], got[phase, side, pair * 2 + 1]], axis=1)
+            return jnp.dot(
+                both, cov[(1 - side) * core + side * (1 - core), pair], preferred_element_type=jnp.float32
+            )
+
+        def direct(q, total):
+            pair = lax.rem(chip // 2 + q, pairs)
+            for h in range(2):
+                origin = pair * 2 + h
+
+                @pl.when(origin != chip)
+                def _():
+                    ag_copy(phase, origin, origin).wait_recv()
+                    forward(phase, origin).start()
+
+            return total + term(0, pair)
+
+        def passed(q, total):
+            pair = lax.rem(chip // 2 + q, pairs)
+            for h in range(2):
+                forward(phase, pair * 2 + h).wait_recv()
+            return total + term(1, pair)
+
+        total = lax.fori_loop(0, pairs, direct, jnp.zeros(weights_ref.shape, jnp.float32))
         if meanwhile is not None:
             meanwhile()
-        row_buf[phase, my_row] = add(n - 1, total)
+        row_buf[phase, my_row] = lax.fori_loop(0, pairs, passed, total)
 
         def send_row(t, carry):
             row_copy(phase, t, my_row).start()
@@ -347,12 +352,12 @@
         return carry
 
     def drain_chip(s, carry):
-        rs_copy(0, logit_send, logit_recv, s - 1).wait_send()
+        to = chip_after(s)
+        rs_copy(0, logit_send, logit_recv, to, chip).wait_send()
         for phase in range(ITERS):
-            rs_copy(phase + 1, resp_send.at[phase], resp_recv.at[phase], s - 1).wait_send()
-        for phase in range(ITERS):
-            ag_copy(phase, s).wait_send()
-            forward(phase, s).wait_send()
+            rs_copy(phase + 1, resp_send.at[phase], resp_recv.at[phase], to, chip).wait_send()
+            ag_copy(phase, to, chip).wait_send()
+            forward(phase, to).wait_send()
         return carry
 
     def drain_col(j, carry):
@@ -367,8 +372,8 @@
         return carry
 
     for phase in range(ITERS):
-        forward(phase, 0).wait_send()
-    lax.fori_loop(0, chips, drain_pair, 0)
+        forward(phase, chip).wait_send()
+    lax.fori_loop(0, pairs, drain_pair, 0)
     lax.fori_loop(1, chips, drain_chip, 0)
     lax.fori_loop(1, n, drain_col, 0)
     lax.fori_loop(1, rows, drain_row, 0)
@@ -377,7 +382,7 @@
 def body(covariates, labels, weights, sample_index):
     users, width = covariates.shape
     n, rows = lax.axis_size("col"), lax.axis_size("row")
-    own, chips = users // n, n // 2
+    own, chips, pairs = users // n, n // 2, n // 4
     classes = weights.shape[0]
     sub = sample_index.shape[0]
     dots = 2 * ITERS - 1
@@ -388,12 +393,12 @@
         in_specs=[pl.BlockSpec(memory_space=pltpu.HBM)] * 4,
         out_specs=[pl.BlockSpec(memory_space=pltpu.VMEM)] * 2,
         scratch_shapes=[
-            pltpu.VMEM((n, own, width), jnp.bfloat16),
+            pltpu.VMEM((2, pairs, 2 * own, width), jnp.bfloat16),
             pltpu.VMEM((1, own), jnp.int32),
             pltpu.VMEM((classes, width), jnp.float32),
             pltpu.VMEM((1, sub), jnp.int32),
-            pltpu.VMEM((ITERS + 1, chips, classes, own), jnp.float32),
-            pltpu.VMEM((ITERS + 1, chips, classes, own), jnp.float32),
+            pltpu.VMEM((ITERS + 1, pairs, classes, 2 * own), jnp.float32),
+            pltpu.VMEM((ITERS + 1, pairs, classes, 2 * own), jnp.float32),
             pltpu.VMEM((chips, classes, own), jnp.float32),
             pltpu.VMEM((chips, classes, own), jnp.float32),
             pltpu.VMEM((ITERS, chips, classes, own), jnp.bfloat16),
@@ -405,7 +410,7 @@
             pltpu.VMEM((dots, 2, 8, LANES), jnp.float32),
             pltpu.VMEM((dots, n, 2, 8, LANES), jnp.float32),
             dma((n,)), dma((3,)),
-            dma((ITERS + 1, chips)), dma((ITERS + 1, chips)),
+            dma((ITERS + 1, pairs)), dma((ITERS + 1, pairs)),
             dma((ITERS + 1, chips)), dma((ITERS + 1, chips)),
             dma((ITERS, chips)), dma((ITERS, chips)),
             dma((ITERS, chips)), dma((ITERS, chips)),
@@ -418,7 +423,7 @@
         ),
         name="newton_step",
     )(
-        covariates.reshape(n, own, width), labels.reshape(n, 1, own), weights, sample_index.reshape(1, sub)
+        covariates.reshape(2, pairs, 2 * own, width), labels.reshape(n, 1, own), weights, sample_index.reshape(1, sub)
     )
     return tuple(out)
 

time: 61.8 us -> 61 us (0.987)
  Pallas kernels: 58.1 us -> 57.3 us
    pallas_call x1, Pallas kernels: 58.1 us -> 57.3 us  [body(): pl.pallas_call(functools.partial(kernel, n, rows, users * rows, sub * row...]
where the time goes in v8:
time: 61 us; the launch traced here: 60.7 us
  Pallas kernels  57.3 us (94%)
  local copies, waits for them, and re-layouts  2.75 us (5%)
  between operations  0.64 us (1%)
    pallas_call x1, Pallas kernels, body(): pl.pallas_call(functools.partial(kernel, n, rows, users * rows, sub * row...  57.3 us
    unnamed x2, local copies, waits for them, and re-layouts  2.75 us

profile of v8, /device:TPU:0, one launch (start us, length us, event | category | flops | bytes accessed | tf_op | source)
XLA Modules:
  0.0 60.7 jit_solution(17865286042191659823)
XLA Ops:
  0.6 57.3 %newton_step.1 = (f32[16,512]{1,0:T(8,128)}, f32[16,512]{1,0:T(8,128)}) custom-call(bf16[2,2,2048,512]{3,2,1,0:T(8,128)(2,1)} %bitcast.3, s32[8,1,1024]{2,1,0:T(1,128)} %bitcast.4, f32[16,512]{1,0:T(8,128)} %weights_hbm.1, s32[1,4096]{1,0:T(1,128)} %bitcast.5), custom_call_target="tpu_custom_call" | custom-call | tf_op jit(solution)/shard_map/newton_step/pallas_call | solution.py:390
  58.0 1.4 %copy.8 = f32[16,512]{1,0:T(8,128)} copy(f32[16,512]{1,0:T(8,128)} %get-tuple-element.4) | data formatting | bytes 65536
  59.3 1.4 %copy.9 = f32[16,512]{1,0:T(8,128)} copy(f32[16,512]{1,0:T(8,128)} %get-tuple-element.5) | data formatting | bytes 65536

commit v9 on v8

--- a/solution.py
+++ b/solution.py
@@ -89,23 +89,22 @@
     lax.fori_loop(1, n, greet_col, 0)
     lax.fori_loop(1, rows, greet_row, 0)
 
-    for copy in small_copies:
-        copy.wait()
-
-    groups = own // LANES
-    padded = max(16, groups)
-    within = index_ref[...] - my_row * (n * own) - own_block * own
-    lane = jnp.bitwise_and(within, LANES - 1)
-    group = jnp.right_shift(within - lane, 7)
-    group_hot = (lax.broadcasted_iota(jnp.int32, (padded, within.shape[1]), 0) == group)
-    lane_hot = (lax.broadcasted_iota(jnp.int32, (LANES, within.shape[1]), 0) == lane)
-    counts = lax.dot_general(
-        group_hot.astype(jnp.float32).astype(jnp.bfloat16), lane_hot.astype(jnp.float32).astype(jnp.bfloat16),
-        (((1,), (1,)), ((), ())), preferred_element_type=jnp.float32,
-    )
-    count = jnp.concatenate([counts[g:g + 1] for g in range(groups)], axis=1)
-
     pl.semaphore_wait(barrier, n - 1 + rows - 1)
+
+    def count_users():
+        small_copies[1].wait()
+        groups = own // LANES
+        padded = max(16, groups)
+        within = index_ref[...] - my_row * (n * own) - own_block * own
+        lane = jnp.bitwise_and(within, LANES - 1)
+        group = jnp.right_shift(within - lane, 7)
+        group_hot = (lax.broadcasted_iota(jnp.int32, (padded, within.shape[1]), 0) == group)
+        lane_hot = (lax.broadcasted_iota(jnp.int32, (LANES, within.shape[1]), 0) == lane)
+        counts = lax.dot_general(
+            group_hot.astype(jnp.float32).astype(jnp.bfloat16), lane_hot.astype(jnp.float32).astype(jnp.bfloat16),
+            (((1,), (1,)), ((), ())), preferred_element_type=jnp.float32,
+        )
+        return jnp.concatenate([counts[g:g + 1] for g in range(groups)], axis=1)
 
     def pair_copy(phase, i):
         return pltpu.make_async_remote_copy(
@@ -186,7 +185,7 @@
             device_id={"row": lax.rem(my_row + t, rows)}, device_id_type=MESH,
         )
 
-    def back_project(phase, values, meanwhile=None):
+    def back_project(phase, values, meanwhile=None, beside=None):
         got[phase, 0, chip] = values
         forward(phase, chip).start()
 
@@ -195,6 +194,9 @@
             return carry
 
         lax.fori_loop(1, chips, send, 0)
+
+        if beside is not None:
+            beside()
 
         def term(side, pair):
             both = jnp.concatenate([got[phase, side, pair * 2], got[phase, side, pair * 2 + 1]], axis=1)
@@ -292,16 +294,19 @@
             total = total + curve_buf[phase, r]
         return total
 
+    small_copies[0].wait()
     weights = weights_ref[...]
     logits = reduce_users(0, weights, logit_send, logit_recv)
     exponent = jnp.exp(logits)
     shares = exponent / jnp.sum(exponent, axis=0, keepdims=True)
+    small_copies[2].wait()
     label = labels_ref[...]
     indicator = (label == lax.broadcasted_iota(jnp.int32, (classes, own), 0)).astype(jnp.float32)
     misfit = (shares - indicator).astype(jnp.bfloat16)
-    gradient = back_project(0, misfit) / user_total + RIDGE_WEIGHT * weights
+    counts = []
+    gradient = back_project(0, misfit, beside=lambda: counts.append(count_users())) / user_total + RIDGE_WEIGHT * weights
     gradient_ref[...] = gradient
-    counted = count * shares
+    counted = counts[0] * shares
 
     residual = -gradient
     direction = residual

time: 61 us -> 61 us (level)
  no operation moved by 1% of the time
where the time goes in v9:
time: 61 us; the launch traced here: 60.7 us
  Pallas kernels  57.3 us (94%)
  local copies, waits for them, and re-layouts  2.75 us (5%)
  between operations  0.64 us (1%)
    pallas_call x1, Pallas kernels, body(): pl.pallas_call(functools.partial(kernel, n, rows, users * rows, sub * row...  57.3 us
    unnamed x2, local copies, waits for them, and re-layouts  2.75 us

profile of v9, /device:TPU:0, one launch (start us, length us, event | category | flops | bytes accessed | tf_op | source)
XLA Modules:
  0.0 60.7 jit_solution(6326557883365046500)
XLA Ops:
  0.6 57.3 %newton_step.1 = (f32[16,512]{1,0:T(8,128)}, f32[16,512]{1,0:T(8,128)}) custom-call(bf16[2,2,2048,512]{3,2,1,0:T(8,128)(2,1)} %bitcast.3, s32[8,1,1024]{2,1,0:T(1,128)} %bitcast.4, f32[16,512]{1,0:T(8,128)} %weights_hbm.1, s32[1,4096]{1,0:T(1,128)} %bitcast.5), custom_call_target="tpu_custom_call" | custom-call | tf_op jit(solution)/shard_map/newton_step/pallas_call | solution.py:395
  58.0 1.4 %copy.8 = f32[16,512]{1,0:T(8,128)} copy(f32[16,512]{1,0:T(8,128)} %get-tuple-element.4) | data formatting | bytes 65536
  59.4 1.4 %copy.9 = f32[16,512]{1,0:T(8,128)} copy(f32[16,512]{1,0:T(8,128)} %get-tuple-element.5) | data formatting | bytes 65536
